TPU v7x, 32 devices: a whole 2x2x4 slice. The times are simulated.
32 devices in a mesh: fsdp: 8 (over z, y), seq: 4 (over x, core).
Axes of the slice: x: 2, y: 2, z: 4, core: 2. Of those that a mesh axis runs over, the one named last changes fastest.
Arguments:
- tokens: bfloat16 [12288, 1024], P(('fsdp', 'seq')), may hold values from -6 to 6
- cotangent: bfloat16 [12288, 1024], P(('fsdp', 'seq')), may hold values from -6 to 6
- ln1_gain: bfloat16 [1024], P('fsdp'), may hold values from 0.099609375 to 1.8984375
- ln1_bias: bfloat16 [1024], P('fsdp'), may hold values from -1.5 to 1.5
- w_qkv: bfloat16 [1024, 3072], P('fsdp'), may hold values from -0.1875 to 0.1875
- b_qv: bfloat16 [2048], P('fsdp'), may hold values from -2.5 to 2.5
- w_out: bfloat16 [1024, 1024], P('fsdp'), may hold values from -0.375 to 0.375
- b_out: bfloat16 [1024], P('fsdp'), may hold values from -1.5 to 1.5
- ln2_gain: bfloat16 [1024], P('fsdp'), may hold values from 0.099609375 to 1.8984375
- ln2_bias: bfloat16 [1024], P('fsdp'), may hold values from -1.5 to 1.5
- w_fc: bfloat16 [1024, 4096], P('fsdp'), may hold values from -0.1875 to 0.1875
- b_fc: bfloat16 [4096], P('fsdp'), may hold values from -2.5 to 2.5
- w_proj: bfloat16 [4096, 1024], P('fsdp'), may hold values from -0.09375 to 0.09375
- b_proj: bfloat16 [1024], P('fsdp'), may hold values from -1.5 to 1.5
Outputs:
- output: bfloat16 [12288, 1024], P(('fsdp', 'seq'))
- grad_tokens: bfloat16 [12288, 1024], P(('fsdp', 'seq'))
- grad_ln1_gain: float32 [1024], P('fsdp')
- grad_ln1_bias: float32 [1024], P('fsdp')
- grad_w_qkv: float32 [1024, 3072], P('fsdp')
- grad_b_qv: float32 [2048], P('fsdp')
- grad_w_out: float32 [1024, 1024], P('fsdp')
- grad_b_out: float32 [1024], P('fsdp')
- grad_ln2_gain: float32 [1024], P('fsdp')
- grad_ln2_bias: float32 [1024], P('fsdp')
- grad_w_fc: float32 [1024, 4096], P('fsdp')
- grad_b_fc: float32 [4096], P('fsdp')
- grad_w_proj: float32 [4096, 1024], P('fsdp')
- grad_b_proj: float32 [1024], P('fsdp')
- rms_values: float32 [3], replicated
All inputs are finite; a program needn't handle non-finite values.
Results may differ from a plain program's by a relative error of at most 0.015.
Values may be sent and summed in bfloat16 or wider, within the bound.
A program may use at most 192 MiB of HBM per device.

v0:
```python
import jax
import jax.numpy as jnp
from jax import lax
from jax.sharding import PartitionSpec as P

BLK = 256
HD = 64


EPSILON = 1e-05


def layer_norm(values, gain_vec, shift):
    centre = values - jnp.mean(values, axis=-1, keepdims=True)
    spread = jnp.mean(centre * centre, axis=-1, keepdims=True)
    return centre * lax.rsqrt(spread + EPSILON) * gain_vec + shift


def gelu_tanh(values):
    return jax.nn.gelu(values, approximate=True)


def block_scores(query_rows, keys_all, block_start, key_block):
    block_rows = query_rows.shape[0]
    scores = jnp.einsum(
        "qhd,khd->hqk", query_rows, keys_all, preferred_element_type=jnp.float32
    ) * HD ** (-0.5)
    query_block = (block_start + jnp.arange(block_rows, dtype=jnp.int32)) // BLK
    allowed = key_block[None, :] <= query_block[:, None]
    return jnp.where(allowed[None], scores, -jnp.inf)


def attend_forward(queries, keys_all, values_all):
    length = queries.shape[0]
    block_rows = min(512, length)
    key_block = jnp.arange(length, dtype=jnp.int32) // BLK

    def one_block(block_start):
        query_rows = lax.dynamic_slice_in_dim(queries, block_start, block_rows, 0)
        scores = block_scores(query_rows, keys_all, block_start, key_block)
        largest = jnp.max(scores, axis=-1, keepdims=True)
        weights = jnp.exp(scores - largest)
        row_total = jnp.sum(weights, axis=-1, keepdims=True)
        soft_probs = (weights / row_total).astype(jnp.bfloat16)
        mixed_block = jnp.einsum(
            "hqk,khd->qhd", soft_probs, values_all, preferred_element_type=jnp.float32
        )
        return (mixed_block.astype(jnp.bfloat16), (largest + jnp.log(row_total))[..., 0])

    starts = jnp.arange(length // block_rows, dtype=jnp.int32) * block_rows
    mixed_blocks, log_total = lax.map(one_block, starts)
    return (mixed_blocks.reshape(length, -1), log_total)


def attend_backward(queries, keys_all, values_all, log_total, grad_mixed):
    length = queries.shape[0]
    block_rows = min(512, length)
    key_block = jnp.arange(length, dtype=jnp.int32) // BLK

    def one_block(running, block_index):
        grad_keys, grad_values = running
        block_start = block_index * block_rows
        query_rows = lax.dynamic_slice_in_dim(queries, block_start, block_rows, 0)
        grad_rows = lax.dynamic_slice_in_dim(grad_mixed, block_start, block_rows, 0)
        scores = block_scores(query_rows, keys_all, block_start, key_block)
        soft_probs = jnp.exp(scores - log_total[block_index][..., None])
        grad_probs = jnp.einsum(
            "qhd,khd->hqk", grad_rows, values_all, preferred_element_type=jnp.float32
        )
        inner_sum = jnp.sum(soft_probs * grad_probs, axis=-1, keepdims=True)
        grad_scores = (soft_probs * (grad_probs - inner_sum)).astype(jnp.bfloat16)
        grad_query = jnp.einsum(
            "hqk,khd->qhd", grad_scores, keys_all, preferred_element_type=jnp.float32
        ) * HD ** (-0.5)
        grad_keys = grad_keys + jnp.einsum(
            "hqk,qhd->khd", grad_scores, query_rows, preferred_element_type=jnp.float32
        ) * HD ** (-0.5)
        grad_values = grad_values + jnp.einsum(
            "hqk,qhd->khd",
            soft_probs.astype(jnp.bfloat16),
            grad_rows,
            preferred_element_type=jnp.float32,
        )
        return ((grad_keys, grad_values), grad_query)

    zero_keys = jnp.zeros(keys_all.shape, jnp.float32)
    block_ids = jnp.arange(length // block_rows, dtype=jnp.int32)
    (grad_keys, grad_values), grad_queries = lax.scan(one_block, (zero_keys, zero_keys), block_ids)
    return (
        grad_queries.reshape(length, -1),
        grad_keys.reshape(length, -1),
        grad_values.reshape(length, -1),
    )


def on_device(
    tokens,
    cotangent,
    ln1_gain,
    ln1_bias,
    w_qkv,
    b_qv,
    w_out,
    b_out,
    ln2_gain,
    ln2_bias,
    w_fc,
    b_fc,
    w_proj,
    b_proj,
):
    gathered = (
        lax.all_gather(ln1_gain, "fsdp", axis=0, tiled=True),
        lax.all_gather(ln1_bias, "fsdp", axis=0, tiled=True),
        lax.all_gather(w_qkv, "fsdp", axis=0, tiled=True),
        lax.all_gather(b_qv, "fsdp", axis=0, tiled=True),
        lax.all_gather(w_out, "fsdp", axis=0, tiled=True),
        lax.all_gather(b_out, "fsdp", axis=0, tiled=True),
        lax.all_gather(ln2_gain, "fsdp", axis=0, tiled=True),
        lax.all_gather(ln2_bias, "fsdp", axis=0, tiled=True),
        lax.all_gather(w_fc, "fsdp", axis=0, tiled=True),
        lax.all_gather(b_fc, "fsdp", axis=0, tiled=True),
        lax.all_gather(w_proj, "fsdp", axis=0, tiled=True),
        lax.all_gather(b_proj, "fsdp", axis=0, tiled=True),
    )
    (
        gain_one,
        shift_one,
        weight_qkv,
        bias_qv,
        weight_out,
        bias_out,
        gain_two,
        shift_two,
        weight_fc,
        bias_fc,
        weight_proj,
        bias_proj,
    ) = gathered
    row_count, feature_count = tokens.shape
    cell_count = row_count * feature_count * lax.axis_size("seq") * lax.axis_size("fsdp")
    inputs = tokens.astype(jnp.float32)
    sum_input = jnp.sum(inputs * inputs)
    total_input = lax.psum(sum_input, ("fsdp", "seq"))
    normed_one = layer_norm(
        inputs, gain_one.astype(jnp.float32), shift_one.astype(jnp.float32)
    ).astype(jnp.bfloat16)
    bias_full = jnp.concatenate(
        [
            bias_qv[:feature_count].astype(jnp.float32),
            jnp.zeros((feature_count,), jnp.float32),
            bias_qv[feature_count:].astype(jnp.float32),
        ]
    )
    projected = (
        jnp.dot(normed_one, weight_qkv, preferred_element_type=jnp.float32) + bias_full
    ).astype(jnp.bfloat16)
    by_heads = lax.all_to_all(
        projected.reshape(row_count, 3, feature_count),
        "seq",
        split_axis=2,
        concat_axis=0,
        tiled=True,
    )
    length = by_heads.shape[0]
    head_count = by_heads.shape[2] // HD
    queries = by_heads[:, 0].reshape(length, head_count, HD)
    keys_all = by_heads[:, 1].reshape(length, head_count, HD)
    values_all = by_heads[:, 2].reshape(length, head_count, HD)
    mixed_heads, log_total = attend_forward(queries, keys_all, values_all)
    mixed_tokens = lax.all_to_all(mixed_heads, "seq", split_axis=0, concat_axis=1, tiled=True)
    branch = jnp.dot(
        mixed_tokens, weight_out, preferred_element_type=jnp.float32
    ) + bias_out.astype(jnp.float32)
    middle = inputs + branch
    sum_middle = jnp.sum(middle * middle)
    total_middle = lax.psum(sum_middle, ("fsdp", "seq"))
    normed_two = layer_norm(
        middle, gain_two.astype(jnp.float32), shift_two.astype(jnp.float32)
    ).astype(jnp.bfloat16)
    before = jnp.dot(normed_two, weight_fc, preferred_element_type=jnp.float32) + bias_fc.astype(
        jnp.float32
    )
    activated, gelu_pull = jax.vjp(gelu_tanh, before)
    activated = activated.astype(jnp.bfloat16)
    feed_out = jnp.dot(
        activated, weight_proj, preferred_element_type=jnp.float32
    ) + bias_proj.astype(jnp.float32)
    stream = middle + feed_out
    sum_stream = jnp.sum(stream * stream)
    output = stream.astype(jnp.bfloat16)
    total_stream = lax.psum(sum_stream, ("fsdp", "seq"))
    totals = jnp.stack([total_input, total_middle, total_stream])
    rms_values = jnp.sqrt(totals / float(cell_count))
    regathered = (
        lax.all_gather(ln1_gain, "fsdp", axis=0, tiled=True),
        lax.all_gather(ln1_bias, "fsdp", axis=0, tiled=True),
        lax.all_gather(w_qkv, "fsdp", axis=0, tiled=True),
        lax.all_gather(w_out, "fsdp", axis=0, tiled=True),
        lax.all_gather(ln2_gain, "fsdp", axis=0, tiled=True),
        lax.all_gather(ln2_bias, "fsdp", axis=0, tiled=True),
        lax.all_gather(w_fc, "fsdp", axis=0, tiled=True),
        lax.all_gather(w_proj, "fsdp", axis=0, tiled=True),
    )
    gain_one, shift_one, weight_qkv, weight_out, gain_two, shift_two, weight_fc, weight_proj = (
        regathered
    )
    grad_out = cotangent.astype(jnp.float32)
    grad_bias_proj = jnp.sum(grad_out, axis=0)
    grad_weight_proj = jnp.einsum(
        "tf,td->fd", activated, cotangent, preferred_element_type=jnp.float32
    )
    grad_act = jnp.einsum("td,fd->tf", cotangent, weight_proj, preferred_element_type=jnp.float32)
    grad_before = gelu_pull(grad_act)[0].astype(jnp.bfloat16)
    grad_bias_fc = jnp.sum(grad_before, axis=0, dtype=jnp.float32)
    grad_weight_fc = jnp.einsum(
        "td,tf->df", normed_two, grad_before, preferred_element_type=jnp.float32
    )
    grad_normed_two = jnp.einsum(
        "tf,df->td", grad_before, weight_fc, preferred_element_type=jnp.float32
    )
    unused_two, pull_two = jax.vjp(
        layer_norm, middle, gain_two.astype(jnp.float32), shift_two.astype(jnp.float32)
    )
    grad_mid_norm, grad_gain_two, grad_shift_two = pull_two(grad_normed_two)
    grad_middle = grad_out + grad_mid_norm
    grad_branch = grad_middle.astype(jnp.bfloat16)
    grad_bias_out = jnp.sum(grad_branch, axis=0, dtype=jnp.float32)
    grad_weight_out = jnp.einsum(
        "ti,td->id", mixed_tokens, grad_branch, preferred_element_type=jnp.float32
    )
    grad_mixed = jnp.einsum(
        "td,id->ti", grad_branch, weight_out, preferred_element_type=jnp.float32
    ).astype(jnp.bfloat16)
    grad_heads = lax.all_to_all(grad_mixed, "seq", split_axis=1, concat_axis=0, tiled=True)
    grad_queries, grad_keys, grad_values = attend_backward(
        queries, keys_all, values_all, log_total, grad_heads.reshape(length, head_count, HD)
    )
    stacked = jnp.stack([grad_queries, grad_keys, grad_values], axis=1).astype(jnp.bfloat16)
    grad_projected = lax.all_to_all(
        stacked, "seq", split_axis=0, concat_axis=2, tiled=True
    ).reshape(row_count, 3 * feature_count)
    grad_bias_qv = jnp.concatenate(
        [
            jnp.sum(grad_projected[:, :feature_count], axis=0, dtype=jnp.float32),
            jnp.sum(grad_projected[:, 2 * feature_count :], axis=0, dtype=jnp.float32),
        ]
    )
    grad_weight_qkv = jnp.einsum(
        "td,te->de", normed_one, grad_projected, preferred_element_type=jnp.float32
    )
    grad_normed_one = jnp.einsum(
        "te,de->td", grad_projected, weight_qkv, preferred_element_type=jnp.float32
    )
    unused_one, pull_one = jax.vjp(
        layer_norm, inputs, gain_one.astype(jnp.float32), shift_one.astype(jnp.float32)
    )
    grad_in_norm, grad_gain_one, grad_shift_one = pull_one(grad_normed_one)
    grad_tokens = (grad_middle + grad_in_norm).astype(jnp.bfloat16)
    shared = (
        lax.psum_scatter(
            grad_gain_one.astype(jnp.bfloat16), "fsdp", scatter_dimension=0, tiled=True
        ).astype(jnp.float32),
        lax.psum_scatter(
            grad_shift_one.astype(jnp.bfloat16), "fsdp", scatter_dimension=0, tiled=True
        ).astype(jnp.float32),
        lax.psum_scatter(
            grad_weight_qkv.astype(jnp.bfloat16), "fsdp", scatter_dimension=0, tiled=True
        ).astype(jnp.float32),
        lax.psum_scatter(
            grad_bias_qv.astype(jnp.bfloat16), "fsdp", scatter_dimension=0, tiled=True
        ).astype(jnp.float32),
        lax.psum_scatter(
            grad_weight_out.astype(jnp.bfloat16), "fsdp", scatter_dimension=0, tiled=True
        ).astype(jnp.float32),
        lax.psum_scatter(
            grad_bias_out.astype(jnp.bfloat16), "fsdp", scatter_dimension=0, tiled=True
        ).astype(jnp.float32),
        lax.psum_scatter(
            grad_gain_two.astype(jnp.bfloat16), "fsdp", scatter_dimension=0, tiled=True
        ).astype(jnp.float32),
        lax.psum_scatter(
            grad_shift_two.astype(jnp.bfloat16), "fsdp", scatter_dimension=0, tiled=True
        ).astype(jnp.float32),
        lax.psum_scatter(
            grad_weight_fc.astype(jnp.bfloat16), "fsdp", scatter_dimension=0, tiled=True
        ).astype(jnp.float32),
        lax.psum_scatter(
            grad_bias_fc.astype(jnp.bfloat16), "fsdp", scatter_dimension=0, tiled=True
        ).astype(jnp.float32),
        lax.psum_scatter(
            grad_weight_proj.astype(jnp.bfloat16), "fsdp", scatter_dimension=0, tiled=True
        ).astype(jnp.float32),
        lax.psum_scatter(
            grad_bias_proj.astype(jnp.bfloat16), "fsdp", scatter_dimension=0, tiled=True
        ).astype(jnp.float32),
    )
    summed = lax.psum(
        (
            shared[0],
            shared[1],
            shared[2],
            shared[3],
            shared[4],
            shared[5],
            shared[6],
            shared[7],
            shared[8],
            shared[9],
            shared[10],
            shared[11],
        ),
        "seq",
    )
    return (
        output,
        grad_tokens,
        summed[0],
        summed[1],
        summed[2],
        summed[3],
        summed[4],
        summed[5],
        summed[6],
        summed[7],
        summed[8],
        summed[9],
        summed[10],
        summed[11],
        rms_values,
    )


def solution(mesh):
    in_specs = (
        P(("fsdp", "seq"), None),
        P(("fsdp", "seq"), None),
        P("fsdp"),
        P("fsdp"),
        P("fsdp", None),
        P("fsdp"),
        P("fsdp", None),
        P("fsdp"),
        P("fsdp"),
        P("fsdp"),
        P("fsdp", None),
        P("fsdp"),
        P("fsdp", None),
        P("fsdp"),
    )
    out_specs = (
        P(("fsdp", "seq"), None),
        P(("fsdp", "seq"), None),
        P("fsdp"),
        P("fsdp"),
        P("fsdp", None),
        P("fsdp"),
        P("fsdp", None),
        P("fsdp"),
        P("fsdp"),
        P("fsdp"),
        P("fsdp", None),
        P("fsdp"),
        P("fsdp", None),
        P("fsdp"),
        P(),
    )
    return jax.shard_map(
        on_device, mesh=mesh, in_specs=in_specs, out_specs=out_specs, check_vma=False
    )
```

profile of v0, /device:TPU:9, one launch (start us, length us, event | category | flops | bytes accessed | tf_op | source)
XLA Modules:
  0.0 1169.0 jit_solution(10980949843085713096)
XLA Ops:
  10.1 15.1 %all-gather.1 = bf16[8,1,128]{2,1,0:T(2,128)(2,1)S(1)} all-gather(bf16[1,1,128]{2,1,0:T(2,128)(2,1)} %bitcast.165), channel_id=1, replica_groups=mesh['fsdp'=8,'seq'=4] {'fsdp'}, dimensions={0}, use_global_device_ids=true | all-gather | bytes 2304 | tf_op jit(solution)/shard_map/all_gather | solution.py:114
  25.2 12.9 %all-gather = bf16[8,1,128]{2,1,0:T(2,128)(2,1)S(1)} all-gather(bf16[1,1,128]{2,1,0:T(2,128)(2,1)} %bitcast.166), channel_id=1, replica_groups=mesh['fsdp'=8,'seq'=4] {'fsdp'}, dimensions={0}, use_global_device_ids=true | all-gather | bytes 2304 | tf_op jit(solution)/shard_map/all_gather | solution.py:113
  38.1 14.7 %all-gather.2 = bf16[8,1,256]{2,1,0:T(2,128)(2,1)S(1)} all-gather(bf16[1,1,256]{2,1,0:T(2,128)(2,1)S(1)} %reshape.251), channel_id=1, replica_groups=mesh['fsdp'=8,'seq'=4] {'fsdp'}, dimensions={0}, use_global_device_ids=true | all-gather | bytes 4608 | tf_op jit(solution)/shard_map/all_gather | solution.py:116
  53.9 54.4 %all-gather.13.cloned.1.call-done = bf16[1024,3072]{1,0:T(8,128)(2,1)} async-done(((bf16[128,3072]{1,0:T(8,128)(2,1)}), bf16[1024,3072]{1,0:T(8,128)(2,1)}) %all-gather.13.cloned.1.call-update) | async-done | bytes 6291472 | tf_op jit(solution)/shard_map/all_gather | solution.py:115
  127.6 35.5 %all-to-all-done = bf16[384,3,1024]{0,1,2:T(4,128)(2,1)S(1)} async-done(((bf16[384,3,1024]{0,1,2:T(4,128)(2,1)}), bf16[384,3,1024]{0,1,2:T(4,128)(2,1)S(1)}, u32[]{:S(2)}, u32[]{:S(2)}) %all-to-all-start) | async-done | bytes 2359328 | tf_op jit(solution)/shard_map/all_to_all | solution.py:158
  172.1 47.8 %while.32 = (s32[]{:T(128)}, bf16[3,512,4,64]{1,3,2,0:T(8,128)(2,1)}, f32[3,4,512]{2,1,0:T(4,128)S(1)}, s32[3]{0:T(128)S(1)}, bf16[1536,4,64]{0,2,1:T(8,128)(2,1...) while((s32[]{:T(128)}, ...), condition=%wide.region_5.6_spmd.clone, body=%wide.region_2.5_spmd.clone.sunk | while | flops 843991040 | bytes 43073708 | solution.py:51
  233.3 13.6 %all-gather.3 = bf16[8,1,128]{2,1,0:T(2,128)(2,1)S(1)} all-gather(bf16[1,1,128]{2,1,0:T(2,128)(2,1)S(1)} %bitcast.167), channel_id=1, replica_groups=mesh['fsdp'=8,'seq'=4] {'fsdp'}, dimensions={0}, use_global_device_ids=true | all-gather | bytes 2304 | tf_op jit(solution)/shard_map/all_gather | solution.py:118
  246.9 23.4 %all-gather.6 = bf16[8,1,512]{2,1,0:T(2,128)(2,1)S(1)} all-gather(bf16[1,1,512]{2,1,0:T(2,128)(2,1)S(1)} %reshape.259), channel_id=1, replica_groups=mesh['fsdp'=8,'seq'=4] {'fsdp'}, dimensions={0}, use_global_device_ids=true | all-gather | bytes 9216 | tf_op jit(solution)/shard_map/all_gather | solution.py:122
  270.4 12.8 %all-gather.5 = bf16[8,1,128]{2,1,0:T(2,128)(2,1)S(1)} all-gather(bf16[1,1,128]{2,1,0:T(2,128)(2,1)S(1)} %bitcast.168), channel_id=1, replica_groups=mesh['fsdp'=8,'seq'=4] {'fsdp'}, dimensions={0}, use_global_device_ids=true | all-gather | bytes 2304 | tf_op jit(solution)/shard_map/all_gather | solution.py:120
  283.2 13.9 %all-gather.4 = bf16[8,1,128]{2,1,0:T(2,128)(2,1)S(1)} all-gather(bf16[1,1,128]{2,1,0:T(2,128)(2,1)S(1)} %bitcast.169), channel_id=1, replica_groups=mesh['fsdp'=8,'seq'=4] {'fsdp'}, dimensions={0}, use_global_device_ids=true | all-gather | bytes 2304 | tf_op jit(solution)/shard_map/all_gather | solution.py:119
  301.5 9.7 fusion.82
  311.2 97.8 %all-gather.17.cloned.1.call-done = bf16[1024,4096]{1,0:T(8,128)(2,1)} async-done(((bf16[128,4096]{1,0:T(8,128)(2,1)}), bf16[1024,4096]{1,0:T(8,128)(2,1)}) %all-gather.17.cloned.1.call-update) | async-done | bytes 8388624 | tf_op jit(solution)/shard_map/all_gather | solution.py:121
  409.0 13.4 %fusion.75 = (bf16[4096]{0:T(1024)(128)(2,1)}, bf16[384,4096]{1,0:T(8,128)(2,1)S(1)}, f32[384,4096]{1,0:T(8,128)}) fusion(f32[384,4096]{1,0:T(8,128)} %fusion.82, f32[4096]{0:T(1024)S(1)} %bitcast.153, bf16[1024,4096]{1,0:T(8,128)(2,1)} %all-gather.17.cloned.1.call-done, f32[384,1024]{1,0:T(8,128)} %copy-done.11, f32[1024]{0:T(1024)S(1)} %bitcast.162, ...), kind=kOutput, calls=%fused_computation.150 | convolution fusion | flops 3257790464 | bytes 25725952 | tf_op jit(solution)/shard_map/dot_general | solution.py:181
  450.3 117.7 %while.33 = (s32[]{:T(128)}, f32[1536,4,64]{0,2,1:T(8,128)}, f32[1536,4,64]{0,2,1:T(8,128)}, bf16[3,512,4,64]{1,3,2,0:T(8,128)(2,1)}, s32[3]{0:T(128)S(1)}, /*in...) while((s32[]{:T(128)}, f32[1536,4,64]{0,2,1:T(8,128)}, ...), condition=%wide.region_12.13_spmd.clone, body=%wide.region_10.12_spmd.clone.sunk | while | flops 2044479488 | bytes 244638416 | solution.py:88
  577.8 39.7 %all_to_all.68 = bf16[1536,3,256]{2,1,0:T(4,128)(2,1)S(1)} all-to-all(bf16[1536,3,256]{2,1,0:T(4,128)(2,1)S(1)} %copy.85), channel_id=1, replica_groups=mesh['fsdp'=8,'seq'=4] {'seq'}, dimensions={0} | all-to-all | bytes 4718592 | tf_op jit(solution)/shard_map/all_to_all | solution.py:240
  629.3 9.0 convolution_convert_fusion.1
  639.3 10.5 convolution_convert_fusion
  650.5 14.2 %all-gather.7 = bf16[8,1,128]{2,1,0:T(2,128)(2,1)S(1)} all-gather(bf16[1,1,128]{2,1,0:T(2,128)(2,1)S(1)} %bitcast.170), channel_id=1, replica_groups=mesh['fsdp'=8,'seq'=4] {'fsdp'}, dimensions={0}, use_global_device_ids=true | all-gather | bytes 2304 | tf_op jit(solution)/shard_map/all_gather | solution.py:124
  667.2 10.9 multiply_reduce_fusion.1
  685.6 46.6 %all-reduce.8 = (f32[1]{0:T(128)}, f32[1]{0:T(128)}, f32[1]{0:T(128)}) all-reduce(f32[1]{0:T(128)} %bitcast.33, f32[1]{0:T(128)} %bitcast.32, f32[1]{0:T(128)} %bitcast.31), channel_id=1, replica_groups=mesh['fsdp'=8,'seq'=4] {'fsdp','seq'}, use_global_device_ids=true, to_apply=%region_53.54 | all-reduce | flops 3 | bytes 24 | tf_op jit(solution)/shard_map/psum | solution.py:192
  736.2 24.5 %all-reduce.10 = (bf16[1024]{0:T(1024)(128)(2,1)S(1)}, bf16[1024]{0:T(1024)(128)(2,1)S(1)}, bf16[2048]{0:T(1024)(128)(2,1)S(1)}, bf16[1024]{0:T(1024)(128)(2,1)S...) all-reduce(bf16[1024]{0:T(1024)(128)(2,1)S(1)} %get-tuple-element.3, ...), channel_id=2, replica_groups=mesh['fsdp'=8,'seq'=4] {'fsdp'}, use_global_device_ids=true, to_apply=%region_16.17.clone | all-reduce | flops 12288 | bytes 49152
  766.6 129.9 %reduce-scatter.9.cloned.1.call-done = bf16[128,4096]{1,0:T(8,128)(2,1)} async-done(((bf16[1024,4096]{1,0:T(8,128)(2,1)}), bf16[128,4096]{1,0:T(8,128)(2,1)}) %reduce-scatter.9.cloned.1.call-update) | async-done | bytes 1048592 | tf_op jit(solution)/shard_map/reduce_scatter | solution.py:285
  896.5 152.2 %reduce-scatter.11.cloned.1.call-done = bf16[512,1024]{1,0:T(8,128)(2,1)} async-done(((bf16[4096,1024]{1,0:T(8,128)(2,1)}), bf16[512,1024]{1,0:T(8,128)(2,1)}) %reduce-scatter.11.cloned.1.call-update) | async-done | bytes 1048592 | tf_op jit(solution)/shard_map/reduce_scatter | solution.py:291
  1048.7 113.3 %all-reduce.12 = (f32[128]{0:T(128)}, f32[128]{0:T(128)}, f32[128,3072]{1,0:T(8,128)}, f32[256]{0:T(256)}, f32[128,1024]{1,0:T(8,128)}, /*index=5*/f32[128]{0:T(...) all-reduce(f32[128]{0:T(128)S(1)} %get-tuple-element.438, ...), channel_id=1, replica_groups=mesh['fsdp'=8,'seq'=4] {'seq'}, use_global_device_ids=true, to_apply=%region_17.18 | all-reduce | flops 1574400 | bytes 9449472 | tf_op jit(solution)/shard_map/psum | solution.py:298
  (342 shorter events, 270.1 us)
Async XLA Ops:
  7.2 101.1 %all-gather.13.cloned.1.call-start = ((), (), s32[]{:S(2)}) async-start(), calls=%async_computation.8 | async-start | bytes 7077888 | tf_op jit(solution)/shard_map/all_gather | solution.py:115
  7.9 289.1 %all-gather.15.cloned.1.call-start = ((), (), s32[]{:S(2)}) async-start(), calls=%async_computation.9 | async-start | bytes 2359296 | tf_op jit(solution)/shard_map/all_gather | solution.py:117
  8.7 292.8 %all-gather.19.cloned.1.call-start = ((), (), s32[]{:S(2)}) async-start(), calls=%async_computation.11 | async-start | bytes 9437184 | tf_op jit(solution)/shard_map/all_gather | solution.py:123
  25.2 83.1 %copy-start.44 = (f32[8,1,128]{2,1,0:T(1,128)}, f32[8,1,128]{2,1,0:T(1,128)S(1)}, u32[]{:S(2)}) copy-start(f32[8,1,128]{2,1,0:T(1,128)S(1)} %convert_element_type.205) | copy-start | bytes 12292
  38.1 70.2 %copy-start.25 = (f32[8,1,128]{2,1,0:T(1,128)}, f32[8,1,128]{2,1,0:T(1,128)S(1)}, u32[]{:S(2)}) copy-start(f32[8,1,128]{2,1,0:T(1,128)S(1)} %convert_element_type.204) | copy-start | bytes 12292
  53.0 55.3 %copy-start.27 = (f32[384]{0:T(512)}, f32[384]{0:T(512)S(1)}, u32[]{:S(2)}) copy-start(f32[384]{0:T(512)S(1)} %broadcast_multiply_fusion.1) | copy-start | bytes 4612
  53.9 54.4 %copy-start.33 = (f32[384]{0:T(512)}, f32[384]{0:T(512)S(1)}, u32[]{:S(2)}) copy-start(f32[384]{0:T(512)S(1)} %fusion.68) | copy-start | bytes 4612
  121.9 41.2 %all-to-all-start = ((bf16[384,3,1024]{0,1,2:T(4,128)(2,1)}), bf16[384,3,1024]{0,1,2:T(4,128)(2,1)S(1)}, u32[]{:S(2)}, u32[]{:S(2)}) async-start(bf16[384,3,1024]{0,1,2:T(4,128)(2,1)} %copy.74), calls=%async_computation | async-start | bytes 6291456 | tf_op jit(solution)/shard_map/all_to_all | solution.py:158
  127.1 282.0 %all-gather.17.cloned.1.call-start = ((), (), s32[]{:S(2)}) async-start(), calls=%async_computation.10 | async-start | bytes 9437184 | tf_op jit(solution)/shard_map/all_gather | solution.py:121
  222.7 60.5 %copy-start.53 = (bf16[128]{0:T(256)(128)(2,1)S(1)}, bf16[128]{0:T(256)(128)(2,1)}, u32[]{:S(2)}) copy-start(bf16[128]{0:T(256)(128)(2,1)} %param.26) | copy-start | bytes 772
  222.7 74.4 %copy-start.7 = (bf16[384,1024]{1,0:T(8,128)(2,1)S(1)}, bf16[384,1024]{1,0:T(8,128)(2,1)}, u32[]{:S(2)}) copy-start(bf16[384,1024]{1,0:T(8,128)(2,1)} %param.18) | copy-start | bytes 2359300
  228.3 68.7 %all-to-all-start.1 = ((bf16[4,384,256]{1,2,0:T(8,128)(2,1)}), bf16[4,384,256]{1,2,0:T(8,128)(2,1)}, u32[]{:S(2)}, u32[]{:S(2)}) async-start(bf16[4,384,256]{1,2,0:T(8,128)(2,1)} %copy.81), calls=%async_computation.1 | async-start | bytes 1572864 | tf_op jit(solution)/shard_map/all_to_all | solution.py:171
  283.1 125.9 %copy-start.46 = (f32[8,1,128]{2,1,0:T(1,128)}, f32[8,1,128]{2,1,0:T(1,128)S(1)}, u32[]{:S(2)}) copy-start(f32[8,1,128]{2,1,0:T(1,128)S(1)} %convert_element_type.208) | copy-start | bytes 12292
  297.0 129.9 %copy-start.37 = (f32[8,1,128]{2,1,0:T(1,128)}, f32[8,1,128]{2,1,0:T(1,128)S(1)}, u32[]{:S(2)}) copy-start(f32[8,1,128]{2,1,0:T(1,128)S(1)} %convert_element_type.207) | copy-start | bytes 12292
  300.0 126.9 %copy-start.29 = (f32[384]{0:T(512)}, f32[384]{0:T(512)S(1)}, u32[]{:S(2)}) copy-start(f32[384]{0:T(512)S(1)} %broadcast_multiply_fusion) | copy-start | bytes 4612
  301.5 125.5 %copy-start.39 = (f32[384]{0:T(512)}, f32[384]{0:T(512)S(1)}, u32[]{:S(2)}) copy-start(f32[384]{0:T(512)S(1)} %fusion.69) | copy-start | bytes 4612
  431.8 15.3 %all-to-all-start.2 = ((bf16[384,4,256]{2,0,1:T(8,128)(2,1)}), bf16[384,4,256]{2,0,1:T(8,128)(2,1)S(1)}, u32[]{:S(2)}, u32[]{:S(2)}) async-start(bf16[384,4,256]{2,0,1:T(8,128)(2,1)} %bitcast.143), calls=%async_computation.2 | async-start | bytes 1572864 | tf_op jit(solution)/shard_map/all_to_all | solution.py:235
  436.3 330.3 %reduce-scatter.7.cloned.1.call-start = ((), (), s32[]{:S(2)}) async-start(), calls=%async_computation.13 | async-start | bytes 2359296 | tf_op jit(solution)/shard_map/reduce_scatter | solution.py:273
  440.3 326.3 %reduce-scatter.5.cloned.1.call-start = ((), (), s32[]{:S(2)}) async-start(), calls=%async_computation.12 | async-start | bytes 7077888 | tf_op jit(solution)/shard_map/reduce_scatter | solution.py:267
  627.9 268.6 %reduce-scatter.9.cloned.1.call-start = ((), (), s32[]{:S(2)}) async-start(), calls=%async_computation.14 | async-start | bytes 9437184 | tf_op jit(solution)/shard_map/reduce_scatter | solution.py:285
  638.2 410.4 %reduce-scatter.11.cloned.1.call-start = ((), (), s32[]{:S(2)}) async-start(), calls=%async_computation.15 | async-start | bytes 9437184 | tf_op jit(solution)/shard_map/reduce_scatter | solution.py:291
  678.1 55.8 %copy-start.32 = (f32[384]{0:T(512)S(1)}, f32[384]{0:T(512)}, u32[]{:S(2)}) copy-start(f32[384]{0:T(512)} %copy-done.31) | copy-start | bytes 4612
  685.6 78.0 %copy-start.15 = (f32[384,1024]{1,0:T(8,128)S(1)}, f32[384,1024]{1,0:T(8,128)}, u32[]{:S(2)}) copy-start(f32[384,1024]{1,0:T(8,128)} %copy-done.14) | copy-start | bytes 4718596
  685.6 78.0 %copy-start.36 = (f32[384]{0:T(512)S(1)}, f32[384]{0:T(512)}, u32[]{:S(2)}) copy-start(f32[384]{0:T(512)} %copy-done.35) | copy-start | bytes 4612
  (78 other events, 742.3 us)
Sparse Core Ops, SparseCore 0:
  10.2 98.0 all-gather.12
  110.4 48.8 all-gather.14
  161.4 122.2 all-gather.18
  285.7 123.2 all-gather.16
  440.9 65.7 reduce-scatter.6
  628.0 117.1 reduce-scatter.4
  748.8 147.6 reduce-scatter.8
  900.6 148.0 reduce-scatter.10
where the time goes:
time: 1180 us; the launch traced here: 1170 us
  waiting for transfers between devices  479 us (41%)
  blocking collectives  345 us (29%)
  matrix products  198 us (17%)
  local copies, waits for them, and re-layouts  56.3 us (5%)
  other arithmetic  45.2 us (4%)
  between operations  16.9 us (1%)
  starting transfers between devices  15.5 us (1%)
  loops' own time  14.3 us (1%)
    reduce_scatter x1, waiting for transfers between devices, on_device(): lax.psum_scatter(grad_weight_proj.astype(jnp.bfloat16), 'fsdp', scatter_d...  152 us
    reduce_scatter x1, waiting for transfers between devices, on_device(): lax.psum_scatter(grad_weight_fc.astype(jnp.bfloat16), 'fsdp', scatter_dim...  130 us
    psum x1, blocking collectives, on_device(): lax.psum((shared[0], shared[1], shared[2], shared[3], shared[4], shared[5...  113 us
    all_gather x1, waiting for transfers between devices, on_device(): lax.all_gather(w_fc, 'fsdp', axis=0, tiled=True)  97.8 us
    all_gather x1, waiting for transfers between devices, on_device(): lax.all_gather(w_qkv, 'fsdp', axis=0, tiled=True)  54.4 us
    psum x1, blocking collectives, on_device(): total_stream = lax.psum(sum_stream, ('fsdp', 'seq'))  46.6 us
    all_to_all x1, blocking collectives, on_device(): lax.all_to_all(stacked, 'seq', split_axis=0, concat_axis=2, tiled=True)  39.7 us
    all_to_all x1, waiting for transfers between devices, on_device(): lax.all_to_all(projected.reshape(row_count, 3, feature_count), 'seq', spl...  35.5 us
  transfers between devices with their start and end apart: 11, of which 6 were waited for; matrix products, arithmetic and copies ran while one was open for 22% of the time, Pallas kernels for 0%

commit v1 on v0

v1 whole, which is shorter than its diff:
```python
import functools

import jax
import jax.numpy as jnp
from jax import lax
from jax.experimental import pallas as pl
from jax.experimental.pallas import tpu as pltpu
from jax.sharding import PartitionSpec as P

BLK = 256
HD = 64
EPSILON = 1e-05
MESH = pl.DeviceIdType.MESH
f32, bf16 = jnp.float32, jnp.bfloat16

def geometry():
    F, S = lax.axis_size("fsdp"), lax.axis_size("seq")
    H = 4 if F % 4 == 0 else 1
    L = F // H
    X = S // 2
    return F, S, H, L, X

class Place:
    def __init__(self):
        self.F, self.S, self.H, self.L, self.X = geometry()
        self.f, self.s = lax.axis_index("fsdp"), lax.axis_index("seq")
        self.h, self.l = self.f // self.L, self.f % self.L
        self.x, self.c = self.s // 2, self.s % 2
    def shard(self, k, j):
        return lax.rem(self.h + self.H - k, self.H) * self.L + lax.rem(self.l + self.L - j, self.L)
    def hi(self, k):
        return (lax.rem(self.h + k, self.H) * self.L + self.l, self.s)
    def lo(self, j):
        return (self.h * self.L + lax.rem(self.l + j, self.L), self.s)
    def across(self, i):
        return (self.f, lax.rem(self.x + i, self.X) * 2 + self.c)
    def sibling(self):
        return (self.f, self.x * 2 + 1 - self.c)
    def everyone(self):
        return ([self.hi(k) for k in range(1, self.H)] + [self.lo(j) for j in range(1, self.L)]
                + [self.across(i) for i in range(1, self.X)] + [self.sibling()])

def greet(place):
    barrier = pltpu.get_barrier_semaphore()
    peers = place.everyone()
    for peer in peers:
        pl.semaphore_signal(barrier, inc=1, device_id=peer, device_id_type=MESH)
    pl.semaphore_wait(barrier, len(peers))

def ag_kernel(count, *refs):
    shards, small = refs[:count], refs[count]
    wholes, smalls = refs[count + 1:2 * count + 1], refs[2 * count + 1]
    own_sem, send_sem, hi_sem, lo_sem, x_sem, core_sem, sm_hi_sem, sm_lo_sem = refs[2 * count + 2:]
    p = Place()
    greet(p)
    sent = []
    def push(src, dst, sem, peer):
        cp = pltpu.make_async_remote_copy(src_ref=src, dst_ref=dst, send_sem=send_sem.at[0], recv_sem=sem, device_id=peer, device_id_type=MESH)
        cp.start(); sent.append(cp)
    def arrived(dst, sem):
        pltpu.make_async_copy(dst, dst, sem).wait()
    width = 5 - p.X
    only = p.x * (3 // (p.X - 1)) if p.X > 1 else 0
    def cols(w, start, n):
        C = shards[w].shape[-1]
        return pl.ds(pl.multiple_of(p.c * (C // 2) + start * (C // 8), 128), n * (C // 8))
    def half(w):
        C = shards[w].shape[-1]
        return pl.ds(pl.multiple_of(p.c * (C // 2), 128), C // 2)
    def other_half(w):
        C = shards[w].shape[-1]
        return pl.ds(pl.multiple_of((1 - p.c) * (C // 2), 128), C // 2)
    own = []
    for w in range(count):
        cp = pltpu.make_async_copy(shards[w], wholes[w].at[p.f], own_sem.at[w]); cp.start(); own.append(cp)
    def start_hi(w):
        mine = cols(w, p.x, width)
        for k in range(1, p.H):
            push(shards[w].at[:, mine], wholes[w].at[p.f, :, mine], hi_sem.at[w, k - 1], p.hi(k))
        for j in range(1, p.L):
            push(shards[w].at[:, mine], wholes[w].at[p.f, :, mine], lo_sem.at[w, j - 1, 0], p.lo(j))
    def pieces():
        return [(j, k) for j in range(p.L) for k in range(p.H) if (j, k) != (0, 0)]
    def after(w, j, k):
        piece = wholes[w].at[p.shard(k, j)]
        for i in range(1, p.X):
            e = cols(w, only, 1)
            push(piece.at[:, e], piece.at[:, e], x_sem.at[w, i - 1, j * p.H + k - 1], p.across(i))
    def finish_hi(w, k):
        mine = cols(w, p.x, width)
        piece = wholes[w].at[p.shard(k, 0), :, mine]
        arrived(piece, hi_sem.at[w, k - 1])
        for j in range(1, p.L):
            push(piece, piece, lo_sem.at[w, j - 1, k], p.lo(j))
        after(w, 0, k)
    def finish_lo(w, k):
        mine = cols(w, p.x, width)
        for j in range(1, p.L):
            arrived(wholes[w].at[p.shard(k, j), :, mine], lo_sem.at[w, j - 1, k])
            after(w, j, k)
    def finish_x(w):
        for (j, k) in pieces():
            for i in range(1, p.X):
                src_x = lax.rem(p.x + p.X - i, p.X)
                e = cols(w, src_x * (3 // (p.X - 1)), 1)
                arrived(wholes[w].at[p.shard(k, j), :, e], x_sem.at[w, i - 1, j * p.H + k - 1])
            piece = wholes[w].at[p.shard(k, j), :, half(w)]
            push(piece, piece, core_sem.at[w, j * p.H + k - 1], p.sibling())
    def finish_core(w):
        for (j, k) in pieces():
            arrived(wholes[w].at[p.shard(k, j), :, other_half(w)], core_sem.at[w, j * p.H + k - 1])
    cp = pltpu.make_async_copy(small, smalls.at[p.f], own_sem.at[count]); cp.start(); own.append(cp)
    for k in range(1, p.H):
        push(small, smalls.at[p.f], sm_hi_sem.at[k - 1], p.hi(k))
    for j in range(1, p.L):
        push(small, smalls.at[p.f], sm_lo_sem.at[j - 1, 0], p.lo(j))
    start_hi(0)
    for k in range(1, p.H):
        piece = smalls.at[p.shard(k, 0)]
        arrived(piece, sm_hi_sem.at[k - 1])
        for j in range(1, p.L):
            push(piece, piece, sm_lo_sem.at[j - 1, k], p.lo(j))
    for t in range(count + 2):
        for k in range(p.H):
            if t < count and k > 0:
                finish_hi(t, k)
            if t + 1 < count and k == 1:
                start_hi(t + 1)
            if 0 < t <= count:
                finish_lo(t - 1, k)
        if 0 < t <= count:
            finish_x(t - 1)
        if 1 < t:
            finish_core(t - 2)
    for j in range(1, p.L):
        for k in range(p.H):
            arrived(smalls.at[p.shard(k, j)], sm_lo_sem.at[j - 1, k])
    for cp in own: cp.wait()
    for cp in sent: cp.wait_send()

def gather_all(shards, small):
    F, S, H, L, X = geometry()
    n = len(shards)
    return pl.pallas_call(
        functools.partial(ag_kernel, n),
        out_shape=[jax.ShapeDtypeStruct((F,) + a.shape, a.dtype) for a in list(shards) + [small]],
        in_specs=[pl.BlockSpec(memory_space=pl.ANY)] * (n + 1),
        out_specs=[pl.BlockSpec(memory_space=pl.ANY)] * (n + 1),
        scratch_shapes=[pltpu.SemaphoreType.DMA((n + 1,)), pltpu.SemaphoreType.DMA((1,)),
            pltpu.SemaphoreType.DMA((n, H - 1)), pltpu.SemaphoreType.DMA((n, L - 1, H)),
            pltpu.SemaphoreType.DMA((n, X - 1, F - 1)), pltpu.SemaphoreType.DMA((n, F - 1)),
            pltpu.SemaphoreType.DMA((H - 1,)), pltpu.SemaphoreType.DMA((L - 1, H))],
        compiler_params=pltpu.CompilerParams(collective_id=1, has_side_effects=True),
    )(*shards, small)


def rs_kernel(n, *refs):
    given, small = refs[:n], refs[n]
    outs, small_out = refs[n + 1:2 * n + 1], refs[2 * n + 1]
    rest = list(refs[2 * n + 2:])
    def take(k):
        got = rest[:k]; del rest[:k]; return got
    parts, from_x, from_lo, from_hi, value, from_x_end, half_out = (take(n) for _ in range(7))
    sm_core, sm_x, sm_sum, sm_lo, sm_hi = take(5)
    load_sem, send_sem, x_sem, lo_sem, hi_sem, end_sem, out_sem, core_sem, sm_sem, smx_sem, smlo_sem, smhi_sem = rest
    loads = [pltpu.make_async_copy(given[w], parts[w], load_sem.at[w]) for w in range(n)]
    for load in loads: load.start()
    p = Place()
    greet(p)
    H, L, X = p.H, p.L, p.X
    width = 5 - X
    step = 3 // (X - 1) if X > 1 else 0
    sent = []
    def push(src, dst, sem, peer):
        cp = pltpu.make_async_remote_copy(src_ref=src, dst_ref=dst, send_sem=send_sem.at[0], recv_sem=sem, device_id=peer, device_id_type=MESH)
        cp.start(); sent.append(cp)
    def arrived(dst, sem):
        pltpu.make_async_copy(dst, dst, sem).wait()
    def unit(w): return parts[w].shape[-1] // 4
    def span(w, start, count):
        return pl.ds(pl.multiple_of(start * unit(w), 128), count * unit(w))
    def other_x(i): return lax.rem(p.x + i, X)
    def shard(k, j):
        return lax.rem(p.h + k, H) * L + lax.rem(p.l + j, L)
    def s1(w):
        loads[w].wait()
        for j in list(range(1, L)) + [0]:
            for k in range(H):
                for i in range(1, X):
                    f = shard(k, j)
                    push(parts[w].at[f, :, span(w, other_x(i) * step, 1)], from_x[w].at[i - 1, f], x_sem.at[w, i - 1, j * H + k], p.across(i))
    def add_x(w, k, j):
        f = shard(k, j)
        for i in range(1, X):
            arrived(from_x[w].at[i - 1, f], x_sem.at[w, i - 1, j * H + k])
        if X > 1:
            cols = span(w, p.x * step, 1)
            total = parts[w][f, :, cols].astype(f32)
            for i in range(1, X):
                total = total + from_x[w][i - 1, f].astype(f32)
            parts[w][f, :, cols] = total.astype(bf16)
    def s2(w):
        for j in range(1, L):
            for k in list(range(1, H)) + [0]:
                add_x(w, k, j)
                f = shard(k, j)
                push(parts[w].at[f, :, span(w, p.x, width)], from_lo[w].at[j - 1, lax.rem(p.h + k, H)], lo_sem.at[w, j - 1, k], p.lo(j))
    def s3(w):
        for k in list(range(1, H)) + [0]:
            add_x(w, k, 0)
            h = lax.rem(p.h + k, H)
            f = h * L + p.l
            cols = span(w, p.x, width)
            total = parts[w][f, :, cols].astype(f32)
            for j in range(1, L):
                arrived(from_lo[w].at[j - 1, h], lo_sem.at[w, j - 1, k])
                total = total + from_lo[w][j - 1, h].astype(f32)
            parts[w][f, :, cols] = total.astype(bf16)
            if k > 0:
                push(parts[w].at[f, :, cols], from_hi[w].at[k - 1], hi_sem.at[w, k - 1], p.hi(k))
    def s4(w):
        cols = span(w, p.x, width)
        total = parts[w][p.f, :, cols].astype(f32)
        for k in range(1, H):
            arrived(from_hi[w].at[k - 1], hi_sem.at[w, k - 1])
            total = total + from_hi[w][k - 1].astype(f32)
        value[w][:, cols] = total.astype(bf16)
        for i in range(1, X):
            push(value[w].at[:, cols], from_x_end[w].at[i - 1, :, cols], end_sem.at[w, i - 1], p.across(i))
    def s5(w):
        mine = span(w, p.x * step, 1)
        half_out[w][:, mine] = value[w][:, mine].astype(f32)
        for i in range(1, X):
            src = lax.rem(p.x + X - i, X)
            cols = span(w, src, width)
            arrived(from_x_end[w].at[i - 1, :, cols], end_sem.at[w, i - 1])
            theirs = span(w, src * step, 1)
            half_out[w][:, theirs] = from_x_end[w][i - 1, :, theirs].astype(f32)
        if X < 4:
            both = pl.ds(unit(w), (4 - X) * unit(w))
            total = value[w][:, both].astype(f32)
            for i in range(1, X):
                total = total + from_x_end[w][i - 1, :, both].astype(f32)
            half_out[w][:, both] = total
        there = outs[w].at[:, pl.ds(pl.multiple_of(p.c * 4 * unit(w), 128), 4 * unit(w))]
        push(half_out[w], there, core_sem.at[w], p.sibling())
        pltpu.make_async_copy(half_out[w], there, out_sem.at[w]).start()
    def s6(w):
        arrived(half_out[w], core_sem.at[w])
        arrived(half_out[w], out_sem.at[w])
    def t0():
        push(small, sm_core, sm_sem.at[0], p.sibling())
    def t1():
        arrived(sm_core, sm_sem.at[0])
        sm_x[p.x] = small[...] + sm_core[...]
        for i in range(1, X):
            push(sm_x.at[p.x], sm_x.at[p.x], smx_sem.at[i - 1], p.across(i))
    def t2():
        for i in range(1, X):
            arrived(sm_x.at[lax.rem(p.x + X - i, X)], smx_sem.at[i - 1])
        total = sm_x[0]
        for i in range(1, X): total = total + sm_x[i]
        sm_sum[...] = total
        for j in range(1, L):
            for k in range(H):
                h = lax.rem(p.h + k, H)
                push(sm_sum.at[shard(k, j)], sm_lo.at[j - 1, h], smlo_sem.at[j - 1, k], p.lo(j))
    def t3():
        for k in range(H):
            h = lax.rem(p.h + k, H)
            f = h * L + p.l
            total = sm_sum[f]
            for j in range(1, L):
                arrived(sm_lo.at[j - 1, h], smlo_sem.at[j - 1, k])
                total = total + sm_lo[j - 1, h]
            sm_core[f] = total
            if k > 0:
                push(sm_core.at[f], sm_hi.at[k - 1], smhi_sem.at[k - 1], p.hi(k))
    def t4():
        total = sm_core[p.f]
        for k in range(1, H):
            arrived(sm_hi.at[k - 1], smhi_sem.at[k - 1])
            total = total + sm_hi[k - 1]
        small_out[...] = total
    s1(0)
    stages = [s2, s3, s4, s5]
    for t in range(n + 3):
        for d, stage in enumerate(stages):
            if 0 <= t - d < n: stage(t - d)
            if d == 0 and t + 1 < n: s1(t + 1)
        if t == 0: t0()
        if t == 1: t1()
        if t == 2: t2()
        if t == 3: t3()
        if t == 4: t4()
    for w in range(n): s6(w)
    for cp in sent: cp.wait_send()

def reduce_all(parts, small):
    F, S, H, L, X = geometry()
    n = len(parts)
    width = 5 - X
    V = pltpu.VMEM
    def each(shape_of, dt):
        return [V(shape_of(a.shape[1], a.shape[2] // 4), dt) for a in parts]
    D = pltpu.SemaphoreType.DMA
    lead = max(X - 1, 1)
    res = pl.pallas_call(
        functools.partial(rs_kernel, n),
        out_shape=[jax.ShapeDtypeStruct((a.shape[1], 2 * a.shape[2]), f32) for a in parts] + [jax.ShapeDtypeStruct(small.shape[1:], f32)],
        in_specs=[pl.BlockSpec(memory_space=pl.ANY)] * n + [pl.BlockSpec(memory_space=pltpu.VMEM)],
        out_specs=[pl.BlockSpec(memory_space=pl.ANY)] * n + [pl.BlockSpec(memory_space=pltpu.VMEM)],
        scratch_shapes=[V(a.shape, bf16) for a in parts] + each(lambda r, u: (lead, F, r, u), bf16) + each(lambda r, u: (L - 1, H, r, width * u), bf16)
          + each(lambda r, u: (H - 1, r, width * u), bf16) + each(lambda r, u: (r, 4 * u), bf16) + each(lambda r, u: (lead, r, 4 * u), bf16)
          + each(lambda r, u: (r, 4 * u), f32)
          + [V(small.shape, f32), V((X,) + small.shape, f32), V(small.shape, f32), V((L - 1, H) + small.shape[1:], f32), V((H - 1,) + small.shape[1:], f32)]
          + [D((n,)), D((1,)), D((n, lead, F)), D((n, L - 1, H)), D((n, H - 1)), D((n, lead)), D((n,)), D((n,)), D((1,)), D((lead,)), D((L - 1, H)), D((H - 1,))],
        compiler_params=pltpu.CompilerParams(collective_id=2, has_side_effects=True, vmem_limit_bytes=60 * 2**20),
    )(*parts, small)
    return res[:n], res[n]


def layer_norm(values, gain_vec, shift):
    centre = values - jnp.mean(values, axis=-1, keepdims=True)
    spread = jnp.mean(centre * centre, axis=-1, keepdims=True)
    return centre * lax.rsqrt(spread + EPSILON) * gain_vec + shift


def gelu_tanh(values):
    return jax.nn.gelu(values, approximate=True)


def block_scores(query_rows, keys_all, block_start, key_block):
    block_rows = query_rows.shape[0]
    scores = jnp.einsum(
        "qhd,khd->hqk", query_rows, keys_all, preferred_element_type=jnp.float32
    ) * HD ** (-0.5)
    query_block = (block_start + jnp.arange(block_rows, dtype=jnp.int32)) // BLK
    allowed = key_block[None, :] <= query_block[:, None]
    return jnp.where(allowed[None], scores, -jnp.inf)


def attend_forward(queries, keys_all, values_all):
    length = queries.shape[0]
    block_rows = min(512, length)
    key_block = jnp.arange(length, dtype=jnp.int32) // BLK

    def one_block(block_start):
        query_rows = lax.dynamic_slice_in_dim(queries, block_start, block_rows, 0)
        scores = block_scores(query_rows, keys_all, block_start, key_block)
        largest = jnp.max(scores, axis=-1, keepdims=True)
        weights = jnp.exp(scores - largest)
        row_total = jnp.sum(weights, axis=-1, keepdims=True)
        soft_probs = (weights / row_total).astype(jnp.bfloat16)
        mixed_block = jnp.einsum(
            "hqk,khd->qhd", soft_probs, values_all, preferred_element_type=jnp.float32
        )
        return (mixed_block.astype(jnp.bfloat16), (largest + jnp.log(row_total))[..., 0])

    starts = jnp.arange(length // block_rows, dtype=jnp.int32) * block_rows
    mixed_blocks, log_total = lax.map(one_block, starts)
    return (mixed_blocks.reshape(length, -1), log_total)


def attend_backward(queries, keys_all, values_all, log_total, grad_mixed):
    length = queries.shape[0]
    block_rows = min(512, length)
    key_block = jnp.arange(length, dtype=jnp.int32) // BLK

    def one_block(running, block_index):
        grad_keys, grad_values = running
        block_start = block_index * block_rows
        query_rows = lax.dynamic_slice_in_dim(queries, block_start, block_rows, 0)
        grad_rows = lax.dynamic_slice_in_dim(grad_mixed, block_start, block_rows, 0)
        scores = block_scores(query_rows, keys_all, block_start, key_block)
        soft_probs = jnp.exp(scores - log_total[block_index][..., None])
        grad_probs = jnp.einsum(
            "qhd,khd->hqk", grad_rows, values_all, preferred_element_type=jnp.float32
        )
        inner_sum = jnp.sum(soft_probs * grad_probs, axis=-1, keepdims=True)
        grad_scores = (soft_probs * (grad_probs - inner_sum)).astype(jnp.bfloat16)
        grad_query = jnp.einsum(
            "hqk,khd->qhd", grad_scores, keys_all, preferred_element_type=jnp.float32
        ) * HD ** (-0.5)
        grad_keys = grad_keys + jnp.einsum(
            "hqk,qhd->khd", grad_scores, query_rows, preferred_element_type=jnp.float32
        ) * HD ** (-0.5)
        grad_values = grad_values + jnp.einsum(
            "hqk,qhd->khd",
            soft_probs.astype(jnp.bfloat16),
            grad_rows,
            preferred_element_type=jnp.float32,
        )
        return ((grad_keys, grad_values), grad_query)

    zero_keys = jnp.zeros(keys_all.shape, jnp.float32)
    block_ids = jnp.arange(length // block_rows, dtype=jnp.int32)
    (grad_keys, grad_values), grad_queries = lax.scan(one_block, (zero_keys, zero_keys), block_ids)
    return (
        grad_queries.reshape(length, -1),
        grad_keys.reshape(length, -1),
        grad_values.reshape(length, -1),
    )


def on_device(
    tokens, cotangent, ln1_gain, ln1_bias, w_qkv, b_qv, w_out, b_out,
    ln2_gain, ln2_bias, w_fc, b_fc, w_proj, b_proj,
):
    F, S, H, L, X = geometry()
    row_count, D = tokens.shape
    vectors = [ln1_gain, ln1_bias, b_qv, b_out, ln2_gain, ln2_bias, b_fc, b_proj]
    sizes = [v.shape[0] for v in vectors]
    flat = jnp.concatenate(vectors)
    small_rows = -(-flat.shape[0] // 2048) * 16
    flat = jnp.pad(flat, (0, small_rows * 128 - flat.shape[0])).reshape(small_rows, 128)
    weight_qkv, weight_out, weight_fc, weight_proj, smalls = gather_all(
        [w_qkv, w_out, w_fc, w_proj], flat
    )
    weight_qkv, weight_out, weight_fc, weight_proj = (
        a.reshape(-1, a.shape[-1]) for a in (weight_qkv, weight_out, weight_fc, weight_proj)
    )
    smalls = smalls.reshape(F, -1).astype(f32)
    whole_vectors, at = [], 0
    for size in sizes:
        whole_vectors.append(smalls[:, at : at + size].reshape(-1))
        at += size
    gain_one, shift_one, bias_qv, bias_out, gain_two, shift_two, bias_fc, bias_proj = whole_vectors
    cell_count = row_count * D * S * F
    inputs = tokens.astype(f32)
    sum_input = jnp.sum(inputs * inputs)
    normed_one = layer_norm(inputs, gain_one, shift_one).astype(bf16)
    bias_full = jnp.concatenate([bias_qv[:D], jnp.zeros((D,), f32), bias_qv[D:]])
    projected = (
        jnp.dot(normed_one, weight_qkv, preferred_element_type=f32) + bias_full
    ).astype(bf16)
    by_heads = lax.all_to_all(
        projected.reshape(row_count, 3, D), "seq", split_axis=2, concat_axis=0, tiled=True
    )
    length = by_heads.shape[0]
    head_count = by_heads.shape[2] // HD
    queries = by_heads[:, 0].reshape(length, head_count, HD)
    keys_all = by_heads[:, 1].reshape(length, head_count, HD)
    values_all = by_heads[:, 2].reshape(length, head_count, HD)
    mixed_heads, log_total = attend_forward(queries, keys_all, values_all)
    mixed_tokens = lax.all_to_all(mixed_heads, "seq", split_axis=0, concat_axis=1, tiled=True)
    middle = inputs + jnp.dot(mixed_tokens, weight_out, preferred_element_type=f32) + bias_out
    sum_middle = jnp.sum(middle * middle)
    normed_two = layer_norm(middle, gain_two, shift_two).astype(bf16)
    before = jnp.dot(normed_two, weight_fc, preferred_element_type=f32) + bias_fc
    activated, gelu_pull = jax.vjp(gelu_tanh, before)
    activated = activated.astype(bf16)
    feed_out = jnp.dot(activated, weight_proj, preferred_element_type=f32) + bias_proj
    stream = middle + feed_out
    sum_stream = jnp.sum(stream * stream)
    output = stream.astype(bf16)
    grad_out = cotangent.astype(f32)
    grad_bias_proj = jnp.sum(grad_out, axis=0)
    grad_act = jnp.einsum("td,fd->tf", cotangent, weight_proj, preferred_element_type=f32)
    grad_before = gelu_pull(grad_act)[0].astype(bf16)
    grad_bias_fc = jnp.sum(grad_before, axis=0, dtype=f32)
    grad_normed_two = jnp.einsum("tf,df->td", grad_before, weight_fc, preferred_element_type=f32)
    _, pull_two = jax.vjp(layer_norm, middle, gain_two, shift_two)
    grad_mid_norm, grad_gain_two, grad_shift_two = pull_two(grad_normed_two)
    grad_middle = grad_out + grad_mid_norm
    grad_branch = grad_middle.astype(bf16)
    grad_bias_out = jnp.sum(grad_branch, axis=0, dtype=f32)
    grad_mixed = jnp.einsum(
        "td,id->ti", grad_branch, weight_out, preferred_element_type=f32
    ).astype(bf16)
    grad_heads = lax.all_to_all(grad_mixed, "seq", split_axis=1, concat_axis=0, tiled=True)
    grad_queries, grad_keys, grad_values = attend_backward(
        queries, keys_all, values_all, log_total, grad_heads.reshape(length, head_count, HD)
    )
    stacked = jnp.stack([grad_queries, grad_keys, grad_values], axis=1).astype(bf16)
    grad_projected = lax.all_to_all(
        stacked, "seq", split_axis=0, concat_axis=2, tiled=True
    ).reshape(row_count, 3 * D)
    grad_bias_qv = jnp.concatenate(
        [
            jnp.sum(grad_projected[:, :D], axis=0, dtype=f32),
            jnp.sum(grad_projected[:, 2 * D :], axis=0, dtype=f32),
        ]
    )
    grad_normed_one = jnp.einsum(
        "te,de->td", grad_projected, weight_qkv, preferred_element_type=f32
    )
    _, pull_one = jax.vjp(layer_norm, inputs, gain_one, shift_one)
    grad_in_norm, grad_gain_one, grad_shift_one = pull_one(grad_normed_one)
    grad_tokens = (grad_middle + grad_in_norm).astype(bf16)

    core = lax.axis_index("seq") % 2
    pairs = [(s, s + 1 - 2 * (s % 2)) for s in range(S)]

    def half_grad(rows, columns):
        wide = columns.shape[1] // 2
        mine = lax.dynamic_slice_in_dim(columns, core * wide, wide, 1)
        theirs = lax.dynamic_slice_in_dim(columns, (1 - core) * wide, wide, 1)
        both_rows = jnp.concatenate([rows, lax.ppermute(rows, "seq", pairs)], axis=0)
        both_columns = jnp.concatenate([mine, lax.ppermute(theirs, "seq", pairs)], axis=0)
        grad = jnp.einsum("ta,tb->ab", both_rows, both_columns, preferred_element_type=f32)
        return grad.astype(bf16).reshape(F, -1, wide)

    halves = [
        half_grad(activated, cotangent),
        half_grad(normed_two, grad_before),
        half_grad(mixed_tokens, grad_branch),
        half_grad(normed_one, grad_projected),
    ]
    small_grads = [
        g.reshape(F, -1)
        for g in (
            grad_gain_one, grad_shift_one, grad_bias_qv, grad_bias_out,
            grad_gain_two, grad_shift_two, grad_bias_fc, grad_bias_proj,
        )
    ]
    sums = jnp.stack([sum_input, sum_middle, sum_stream])
    width = sum(sizes) + 3
    total_rows = -(-width // 1024) * 8
    small_grads = jnp.concatenate(
        small_grads
        + [jnp.broadcast_to(sums, (F, 3)), jnp.zeros((F, total_rows * 128 - width), f32)],
        axis=1,
    ).reshape(F, total_rows, 128)
    (grad_w_proj, grad_w_fc, grad_w_out, grad_w_qkv), reduced = reduce_all(halves, small_grads)
    reduced = reduced.reshape(-1)
    vectors_out, at = [], 0
    for size in sizes:
        vectors_out.append(reduced[at : at + size])
        at += size
    rms_values = jnp.sqrt(reduced[at : at + 3] / float(cell_count))
    return (
        output, grad_tokens, vectors_out[0], vectors_out[1], grad_w_qkv, vectors_out[2],
        grad_w_out, vectors_out[3], vectors_out[4], vectors_out[5], grad_w_fc, vectors_out[6],
        grad_w_proj, vectors_out[7], rms_values,
    )


def solution(mesh):
    in_specs = (
        P(("fsdp", "seq"), None),
        P(("fsdp", "seq"), None),
        P("fsdp"),
        P("fsdp"),
        P("fsdp", None),
        P("fsdp"),
        P("fsdp", None),
        P("fsdp"),
        P("fsdp"),
        P("fsdp"),
        P("fsdp", None),
        P("fsdp"),
        P("fsdp", None),
        P("fsdp"),
    )
    out_specs = (
        P(("fsdp", "seq"), None),
        P(("fsdp", "seq"), None),
        P("fsdp"),
        P("fsdp"),
        P("fsdp", None),
        P("fsdp"),
        P("fsdp", None),
        P("fsdp"),
        P("fsdp"),
        P("fsdp"),
        P("fsdp", None),
        P("fsdp"),
        P("fsdp", None),
        P("fsdp"),
        P(),
    )
    return jax.shard_map(
        on_device, mesh=mesh, in_specs=in_specs, out_specs=out_specs, check_vma=False
    )
```

time: 1180 us -> 721 us (0.61)
  waiting for transfers between devices: 479 us -> 67.2 us
  blocking collectives: 345 us -> 0 us
  Pallas kernels: 0 us -> 293 us
  local copies, waits for them, and re-layouts: 56.3 us -> 82.5 us
  between operations: 16.9 us -> 1.72 us
  matrix products: 198 us -> 186 us
    pallas_call x0 -> x2, Pallas kernels: none -> 293 us  [the longest x1 160 us: reduce_all(): pl.pallas_call(functools.partial(rs_kernel, n), out_shape=[jax.ShapeDtype...]
    reduce_scatter x4 -> x0, waiting for transfers between devices: 282 us -> none  [the longest x1 152 us: on_device(): lax.psum_scatter(grad_weight_proj.astype(jnp.bfloat16), 'fsdp', scatter_d...]
    psum x2 -> x0, blocking collectives: 160 us -> none  [the longest x1 113 us: on_device(): lax.psum((shared[0], shared[1], shared[2], shared[3], shared[4], shared[5...]
    all_gather x4 -> x0, waiting for transfers between devices: 152 us -> none  [the longest x1 97.8 us: on_device(): lax.all_gather(w_fc, 'fsdp', axis=0, tiled=True)]
    all_gather x8 -> x0, blocking collectives: 121 us -> none  [the longest x1 23.4 us: on_device(): lax.all_gather(b_fc, 'fsdp', axis=0, tiled=True)]
    all_to_all x1 -> x0, blocking collectives: 39.7 us -> none  [on_device(): lax.all_to_all(stacked, 'seq', split_axis=0, concat_axis=2, tiled=True)]
    unnamed x1 -> x0, blocking collectives: 24.5 us -> none
    all_to_all x1 -> x2, waiting for transfers between devices: 35.5 us -> 51.4 us  [the longest x1 36 us: on_device(): lax.all_to_all(projected.reshape(row_count, 3, D), 'seq', split_axis=2, c...]
  transfers between devices with their start and end apart: 11 -> 12, of which waited for: 6 -> 4; matrix products, arithmetic and copies ran while one was open for 22% -> 24% of each run, Pallas kernels for 0% -> 0%
where the time goes in v1:
time: 721 us; the launch traced here: 714 us
  Pallas kernels  293 us (41%)
  matrix products  186 us (26%)
  local copies, waits for them, and re-layouts  82.5 us (11%)
  waiting for transfers between devices  67.2 us (9%)
  other arithmetic  46 us (6%)
  starting transfers between devices  23.1 us (3%)
  loops' own time  14.3 us (2%)
    pallas_call x1, Pallas kernels, reduce_all(): pl.pallas_call(functools.partial(rs_kernel, n), out_shape=[jax.ShapeDtype...  160 us
    pallas_call x1, Pallas kernels, gather_all(): pl.pallas_call(functools.partial(ag_kernel, n), out_shape=[jax.ShapeDtype...  133 us
    all_to_all x1, waiting for transfers between devices, on_device(): lax.all_to_all(projected.reshape(row_count, 3, D), 'seq', split_axis=2, c...  36 us
    dot_general x6, matrix products, block_scores(): jnp.einsum('qhd,khd->hqk', query_rows, keys_all, preferred_element_type=j...  33.6 us
    dot_general x4, matrix products, half_grad(): jnp.einsum('ta,tb->ab', both_rows, both_columns, preferred_element_type=f32)  24.9 us
    dot_general x3, matrix products, one_block(): jnp.einsum('qhd,khd->hqk', grad_rows, values_all, preferred_element_type=...  19.1 us
    dot_general x3, matrix products, one_block(): jnp.einsum('hqk,qhd->khd', soft_probs.astype(jnp.bfloat16), grad_rows, pr...  18.5 us
    dot_general x3, matrix products, one_block(): jnp.einsum('hqk,qhd->khd', grad_scores, query_rows, preferred_element_typ...  16.9 us
  transfers between devices with their start and end apart: 12, of which 4 were waited for; matrix products, arithmetic and copies ran while one was open for 24% of the time, Pallas kernels for 0%

profile of v1, /device:TPU:9, one launch (start us, length us, event | category | flops | bytes accessed | tf_op | source)
XLA Modules:
  0.0 713.8 jit_solution(6095427602463099759)
XLA Ops:
  8.0 132.7 %shard_map.253 = (bf16[8,128,3072]{2,1,0:T(8,128)(2,1)}, bf16[8,128,1024]{2,1,0:T(8,128)(2,1)}, bf16[8,128,4096]{2,1,0:T(8,128)(2,1)}, bf16[8,512,1024]{2,1,0:T(8,128)(2,1)}, bf16[8,16,128]{2,1,0:T(8,128)(2,1)}) custom-call(bf16[128,3072]{1,0:T(8,128)(2,1)} %refs_0_.1, bf16[128,1024]{1,0:T(8,128)(2,1)} %refs_1_.1, bf16[128,4096]{1,0:T(8,128)(2,1)} %refs_2_.1, ...), custom_call_target="tpu_custom_call" | custom-call | tf_op jit(solution)/shard_map/pallas_call | solution.py:144
  144.0 6.6 add_convert_fusion
  161.3 36.0 %all-to-all-done = bf16[384,3,1024]{0,1,2:T(4,128)(2,1)S(1)} async-done(((bf16[384,3,1024]{0,1,2:T(4,128)(2,1)}), bf16[384,3,1024]{0,1,2:T(4,128)(2,1)S(1)}, u32[]{:S(2)}, u32[]{:S(2)}) %all-to-all-start) | async-done | bytes 2359328 | tf_op jit(solution)/shard_map/all_to_all | solution.py:437
  206.2 47.8 %while.32 = (s32[]{:T(128)}, bf16[3,512,4,64]{1,3,2,0:T(8,128)(2,1)}, f32[3,4,512]{2,1,0:T(4,128)S(1)}, s32[3]{0:T(128)S(1)}, bf16[1536,4,64]{0,2,1:T(8,128)(2,1...) while((s32[]{:T(128)}, ...), condition=%wide.region_5.6_spmd.clone, body=%wide.region_2.5_spmd.clone.sunk | while | flops 843991040 | bytes 43073708 | solution.py:361
  267.9 10.8 %all-to-all-done.1 = bf16[4,384,256]{1,2,0:T(8,128)(2,1)} async-done(((bf16[4,384,256]{1,2,0:T(8,128)(2,1)}), bf16[4,384,256]{1,2,0:T(8,128)(2,1)}, u32[]{:S(2)}, u32[]{:S(2)}) %all-to-all-start.1) | async-done | bytes 786464 | tf_op jit(solution)/shard_map/all_to_all | solution.py:446
  282.5 11.2 %multiply_convert_fusion.1 = (bf16[384,4096]{1,0:T(8,128)(2,1)}, f32[384,4096]{1,0:T(8,128)}) fusion(f32[4096]{0:T(1024)S(1)} %bitcast.218, bf16[384,1024]{1,0:T(8,128)(2,1)S(1)} %add_convert_fusion.2, bf16[1024,4096]{1,0:T(8,128)(2,1)} %bitcast.229), kind=kOutput, calls=%fused_computation.93 | convolution fusion | flops 3236954112 | bytes 18628608 | tf_op jit(solution)/shard_map/dot_general | solution.py:450
  293.7 9.8 %convert_reduce_fusion = (f32[4096]{0:T(1024)}, bf16[384,4096]{1,0:T(8,128)(2,1)S(1)}) fusion(f32[384,4096]{1,0:T(8,128)} %get-tuple-element.446, bf16[4096,1024]{1,0:T(8,128)(2,1)S(1)} %bitcast.228, bf16[384,1024]{1,0:T(8,128)(2,1)S(1)} %copy-done.15), kind=kOutput, calls=%fused_computation.92 | convolution fusion | flops 3255824384 | bytes 18628608 | tf_op jit(solution)/shard_map/td,fd->tf/dot_general | solution.py:459
  332.9 117.4 %while.33 = (s32[]{:T(128)}, f32[1536,4,64]{0,2,1:T(8,128)}, f32[1536,4,64]{0,2,1:T(8,128)}, bf16[3,512,4,64]{1,3,2,0:T(8,128)(2,1)}, s32[3]{0:T(128)S(1)}, /*in...) while((s32[]{:T(128)}, f32[1536,4,64]{0,2,1:T(8,128)}, ...), condition=%wide.region_12.13_spmd.clone, body=%wide.region_10.12_spmd.clone.sunk | while | flops 2044479488 | bytes 244638416 | solution.py:398
  334.3 6.4 fusion.172
  343.2 7.7 %multiply_reduce_fusion.7 = (f32[4,512]{1,0:T(4,128)S(1)}, f32[4,512,1536]{2,1,0:T(8,128)S(1)}) fusion(f32[4,512,1536]{2,1,0:T(8,128)} %fusion.172, f32[4,512]{1,0:T(4,128)S(1)} %dynamic-slice_bitcast_fusion.2, bf16[1536,4,64]{0,2,1:T(8,128)(2,1)S(1)} %get-tuple-element.630, bf16[1536,4,64]{0,2,1:T(8,128)(2,1)} %get-tuple-element.629, ...), kind=kOutput, calls=%fused_computation.35.clone.1 | convolution fusion | flops 418379776 | bytes 27017220 | tf_op jit(solution)/shard_map/while/body/eval_jaxpr/qhd,khd->hqk/dot_general | solution.py:335
  362.6 6.2 fusion.174
  373.1 6.4 fusion.172
  382.0 7.7 %multiply_reduce_fusion.7 = (f32[4,512]{1,0:T(4,128)S(1)}, f32[4,512,1536]{2,1,0:T(8,128)S(1)}) fusion(f32[4,512,1536]{2,1,0:T(8,128)} %fusion.172, f32[4,512]{1,0:T(4,128)S(1)} %dynamic-slice_bitcast_fusion.2, bf16[1536,4,64]{0,2,1:T(8,128)(2,1)S(1)} %get-tuple-element.630, bf16[1536,4,64]{0,2,1:T(8,128)(2,1)} %get-tuple-element.629, ...), kind=kOutput, calls=%fused_computation.35.clone.1 | convolution fusion | flops 418379776 | bytes 27017220 | tf_op jit(solution)/shard_map/while/body/eval_jaxpr/qhd,khd->hqk/dot_general | solution.py:335
  401.9 6.2 fusion.174
  412.4 6.4 fusion.172
  421.3 7.7 %multiply_reduce_fusion.7 = (f32[4,512]{1,0:T(4,128)S(1)}, f32[4,512,1536]{2,1,0:T(8,128)S(1)}) fusion(f32[4,512,1536]{2,1,0:T(8,128)} %fusion.172, f32[4,512]{1,0:T(4,128)S(1)} %dynamic-slice_bitcast_fusion.2, bf16[1536,4,64]{0,2,1:T(8,128)(2,1)S(1)} %get-tuple-element.630, bf16[1536,4,64]{0,2,1:T(8,128)(2,1)} %get-tuple-element.629, ...), kind=kOutput, calls=%fused_computation.35.clone.1 | convolution fusion | flops 418379776 | bytes 27017220 | tf_op jit(solution)/shard_map/while/body/eval_jaxpr/qhd,khd->hqk/dot_general | solution.py:335
  441.1 6.2 fusion.174
  460.8 5.8 all-to-all-start.3
  466.9 9.2 %multiply_reduce_fusion.1 = (f32[]{:T(128)}, bf16[384,1024]{1,0:T(8,128)(2,1)}) fusion(f32[384,1024]{1,0:T(8,128)S(1)} %copy-done.10, f32[1024]{0:T(1024)S(1)} %copy-done.44, bf16[384,4096]{1,0:T(8,128)(2,1)} %get-tuple-element.445, bf16[4096,1024]{1,0:T(8,128)(2,1)} %bitcast.225), kind=kOutput, calls=%fused_computation.137 | convolution fusion | flops 3223191552 | bytes 13897732 | tf_op jit(solution)/shard_map/dot_general | solution.py:453
  480.2 7.1 convolution_convert_fusion.1
  487.3 15.4 %all-to-all-done.3 = bf16[1536,3,256]{2,1,0:T(4,128)(2,1)} async-done(((bf16[1536,3,256]{2,1,0:T(4,128)(2,1)}), bf16[1536,3,256]{2,1,0:T(4,128)(2,1)}, u32[]{:S(2)}, u32[]{:S(2)}) %all-to-all-start.3) | async-done | bytes 2359328 | tf_op jit(solution)/shard_map/all_to_all | solution.py:476
  511.7 5.9 fusion.112
  527.3 8.5 %fusion.62 = bf16[4096,512]{1,0:T(8,128)(2,1)} fusion(bf16[384,4096]{1,0:T(8,128)(2,1)} %collective-permute-done, bf16[384,4096]{1,0:T(8,128)(2,1)} %get-tuple-element.445, bf16[384,512]{1,0:T(8,128)(2,1)} %collective-permute-done.1, bf16[384,512]{1,0:T(8,128)(2,1)} %get-tuple-element.427), kind=kOutput, calls=%fused_computation.94 | convolution fusion | flops 3237478400 | bytes 11272192 | tf_op jit(solution)/shard_map/ta,tb->ab/dot_general | solution.py:501
  541.6 160.4 %shard_map.254 = (f32[512,1024]{1,0:T(8,128)}, f32[128,4096]{1,0:T(8,128)}, f32[128,1024]{1,0:T(8,128)}, f32[128,3072]{1,0:T(8,128)}, f32[16,128]{1,0:T(8,128)}) custom-call(bf16[8,512,512]{2,1,0:T(8,128)(2,1)} %bitcast.201, bf16[8,128,2048]{2,1,0:T(8,128)(2,1)} %bitcast.200, bf16[8,128,512]{2,1,0:T(8,128)(2,1)} %bitcast.208, ...), custom_call_target="tpu_custom_call" | custom-call | tf_op jit(solution)/shard_map/pallas_call | solution.py:308
  (333 shorter events, 217.6 us)
Async XLA Ops:
  0.6 141.5 %copy-start.6 = (bf16[384,1024]{1,0:T(8,128)(2,1)S(1)}, bf16[384,1024]{1,0:T(8,128)(2,1)}, u32[]{:S(2)}) copy-start(bf16[384,1024]{1,0:T(8,128)(2,1)} %param.18) | copy-start | bytes 2359300
  157.3 40.0 %all-to-all-start = ((bf16[384,3,1024]{0,1,2:T(4,128)(2,1)}), bf16[384,3,1024]{0,1,2:T(4,128)(2,1)S(1)}, u32[]{:S(2)}, u32[]{:S(2)}) async-start(bf16[384,3,1024]{0,1,2:T(4,128)(2,1)} %copy.74), calls=%async_computation | async-start | bytes 6291456 | tf_op jit(solution)/shard_map/all_to_all | solution.py:437
  256.8 21.9 %copy-start.7 = (bf16[384,1024]{1,0:T(8,128)(2,1)S(1)}, bf16[384,1024]{1,0:T(8,128)(2,1)}, u32[]{:S(2)}) copy-start(bf16[384,1024]{1,0:T(8,128)(2,1)} %param.18) | copy-start | bytes 2359300
  262.4 16.3 %all-to-all-start.1 = ((bf16[4,384,256]{1,2,0:T(8,128)(2,1)}), bf16[4,384,256]{1,2,0:T(8,128)(2,1)}, u32[]{:S(2)}, u32[]{:S(2)}) async-start(bf16[4,384,256]{1,2,0:T(8,128)(2,1)} %copy.81), calls=%async_computation.1 | async-start | bytes 1572864 | tf_op jit(solution)/shard_map/all_to_all | solution.py:446
  278.7 14.9 %slice-start.5 = ((s8[8388608]{0:T(1024)(128)(4,1)}), s8[4194304]{0:T(1024)(128)(4,1)S(1)}, s32[]{:S(2)}) async-start(s8[8388608]{0:T(1024)(128)(4,1)} %bitcast.226), calls=%async_computation.9 | async-start | bytes 8388608
  281.8 26.2 %copy-start.9 = (f32[384,1024]{1,0:T(8,128)}, f32[384,1024]{1,0:T(8,128)S(1)}, u32[]{:S(2)}) copy-start(f32[384,1024]{1,0:T(8,128)S(1)} %get-tuple-element.444) | copy-start | bytes 4718596
  282.4 11.2 %copy-start.30 = (bf16[384,1024]{1,0:T(8,128)(2,1)}, bf16[384,1024]{1,0:T(8,128)(2,1)S(1)}, u32[]{:S(2)}) copy-start(bf16[384,1024]{1,0:T(8,128)(2,1)S(1)} %add_convert_fusion.2) | copy-start | bytes 2359300
  282.5 11.2 %copy-start.15 = (bf16[384,1024]{1,0:T(8,128)(2,1)S(1)}, bf16[384,1024]{1,0:T(8,128)(2,1)}, u32[]{:S(2)}) copy-start(bf16[384,1024]{1,0:T(8,128)(2,1)} %param.19) | copy-start | bytes 2359300
  282.5 11.2 %slice-start.6 = ((s8[8388608]{0:T(1024)(128)(4,1)}), s8[4194304]{0:T(1024)(128)(4,1)S(1)}, s32[]{:S(2)}) async-start(s8[8388608]{0:T(1024)(128)(4,1)} %bitcast.226), calls=%async_computation.10 | async-start | bytes 8388608
  282.5 21.0 %slice-start.7 = ((s8[8388608]{0:T(1024)(128)(4,1)}), s8[4194304]{0:T(1024)(128)(4,1)S(1)}, s32[]{:S(2)}) async-start(s8[8388608]{0:T(1024)(128)(4,1)} %bitcast.230), calls=%async_computation.11 | async-start | bytes 8388608
  293.7 9.8 %slice-start.8 = ((s8[8388608]{0:T(1024)(128)(4,1)}), s8[4194304]{0:T(1024)(128)(4,1)S(1)}, s32[]{:S(2)}) async-start(s8[8388608]{0:T(1024)(128)(4,1)} %bitcast.230), calls=%async_computation.12 | async-start | bytes 8388608
  313.0 16.1 %all-to-all-start.2 = ((bf16[384,4,256]{2,0,1:T(8,128)(2,1)}), bf16[384,4,256]{2,0,1:T(8,128)(2,1)}, u32[]{:S(2)}, u32[]{:S(2)}) async-start(bf16[384,4,256]{2,0,1:T(8,128)(2,1)} %bitcast.202), calls=%async_computation.2 | async-start | bytes 1572864 | tf_op jit(solution)/shard_map/all_to_all | solution.py:471
  318.2 217.6 %collective-permute-start.6 = (bf16[384,1024]{1,0:T(8,128)(2,1)}, bf16[384,1024]{1,0:T(8,128)(2,1)}, u32[]{:S(2)}, u32[]{:S(2)}) collective-permute-start(bf16[384,1024]{1,0:T(8,128)(2,1)} %copy-done.28), channel_id=1, source_target_pairs={{0,1},{1,0},{2,3},{3,2},{4,5},{5,4},{6,7},{7,6},{8,9},{9,8},{10,11... | collective-permute-start | bytes 2359304 | tf_op jit(solution)/shard_map/ppermute | solution.py:499
  319.3 160.9 %collective-permute-start.2 = (bf16[384,1024]{1,0:T(8,128)(2,1)}, bf16[384,1024]{1,0:T(8,128)(2,1)}, u32[]{:S(2)}, u32[]{:S(2)}) collective-permute-start(bf16[384,1024]{1,0:T(8,128)(2,1)} %copy-done.30), channel_id=1, source_target_pairs={{0,1},{1,0},{2,3},{3,2},{4,5},{5,4},{6,7},{7,6},{8,9},{9,8},{10,11... | collective-permute-start | bytes 2359304 | tf_op jit(solution)/shard_map/ppermute | solution.py:499
  319.8 156.9 %collective-permute-start.4 = (bf16[384,1024]{0,1:T(8,128)(2,1)}, bf16[384,1024]{0,1:T(8,128)(2,1)}, u32[]{:S(2)}, u32[]{:S(2)}) collective-permute-start(bf16[384,1024]{0,1:T(8,128)(2,1)} %bitcast.12), channel_id=1, source_target_pairs={{0,1},{1,0},{2,3},{3,2},{4,5},{5,4},{6,7},{7,6},{8,9},{9,8},{10,11... | collective-permute-start | bytes 2359304 | tf_op jit(solution)/shard_map/ppermute | solution.py:499
  323.8 156.4 %collective-permute-start.3 = (bf16[384,2048]{1,0:T(8,128)(2,1)}, bf16[384,2048]{1,0:T(8,128)(2,1)}, u32[]{:S(2)}, u32[]{:S(2)}) collective-permute-start(bf16[384,2048]{1,0:T(8,128)(2,1)} %get-tuple-element.415), channel_id=1, source_target_pairs={{0,1},{1,0},{2,3},{3,2},{4,5},{5,4},{6,7},{7,6},{8,9},{9,8},{10,11... | collective-permute-start | bytes 4718600 | tf_op jit(solution)/shard_map/ppermute | solution.py:500
  357.3 11.6 %slice-start.3 = ((s8[6291456]{0:T(1024)(128)(4,1)}), s8[4194304]{0:T(1024)(128)(4,1)S(1)}, s32[]{:S(2)}) async-start(s8[6291456]{0:T(1024)(128)(4,1)} %bitcast.188), calls=%async_computation.7 | async-start | bytes 8388608 | tf_op jit(solution)/shard_map/while
  396.1 12.0 %slice-start.3 = ((s8[6291456]{0:T(1024)(128)(4,1)}), s8[4194304]{0:T(1024)(128)(4,1)S(1)}, s32[]{:S(2)}) async-start(s8[6291456]{0:T(1024)(128)(4,1)} %bitcast.188), calls=%async_computation.7 | async-start | bytes 8388608 | tf_op jit(solution)/shard_map/while
  435.3 12.0 %slice-start.3 = ((s8[6291456]{0:T(1024)(128)(4,1)}), s8[4194304]{0:T(1024)(128)(4,1)S(1)}, s32[]{:S(2)}) async-start(s8[6291456]{0:T(1024)(128)(4,1)} %bitcast.188), calls=%async_computation.7 | async-start | bytes 8388608 | tf_op jit(solution)/shard_map/while
  460.8 42.0 %all-to-all-start.3 = ((bf16[1536,3,256]{2,1,0:T(4,128)(2,1)}), bf16[1536,3,256]{2,1,0:T(4,128)(2,1)}, u32[]{:S(2)}, u32[]{:S(2)}) async-start(bf16[1536,3,256]{2,1,0:T(4,128)(2,1)} %copy.85), calls=%async_computation.3 | async-start | bytes 6291456 | tf_op jit(solution)/shard_map/all_to_all | solution.py:476
  466.7 9.4 %collective-permute-start.5 = (bf16[384,512]{1,0:T(8,128)(2,1)S(1)}, bf16[384,512]{1,0:T(8,128)(2,1)S(1)}, u32[]{:S(2)}, u32[]{:S(2)}) collective-permute-start(bf16[384,512]{1,0:T(8,128)(2,1)S(1)} %get-tuple-element.426), channel_id=1, source_target_pairs={{0,1},{1,0},{2,3},{3,2},{4,5},{5,4},{6,7},{7,6},{8,9},{9,8},{10,11... | collective-permute-start | bytes 1179656 | tf_op jit(solution)/shard_map/ppermute | solution.py:500
  476.1 51.2 %collective-permute-start.1 = (bf16[384,512]{1,0:T(8,128)(2,1)}, bf16[384,512]{1,0:T(8,128)(2,1)}, u32[]{:S(2)}, u32[]{:S(2)}) collective-permute-start(bf16[384,512]{1,0:T(8,128)(2,1)} %get-tuple-element.428), channel_id=1, source_target_pairs={{0,1},{1,0},{2,3},{3,2},{4,5},{5,4},{6,7},{7,6},{8,9},{9,8},{10,11... | collective-permute-start | bytes 1179656 | tf_op jit(solution)/shard_map/ppermute | solution.py:500
  476.7 50.6 %collective-permute-start = (bf16[384,4096]{1,0:T(8,128)(2,1)}, bf16[384,4096]{1,0:T(8,128)(2,1)}, u32[]{:S(2)}, u32[]{:S(2)}) collective-permute-start(bf16[384,4096]{1,0:T(8,128)(2,1)} %get-tuple-element.445), channel_id=1, source_target_pairs={{0,1},{1,0},{2,3},{3,2},{4,5},{5,4},{6,7},{7,6},{8,9},{9,8},{10,11... | collective-permute-start | bytes 9437192 | tf_op jit(solution)/shard_map/ppermute | solution.py:499
  510.8 25.0 %collective-permute-start.7 = (bf16[384,1536]{0,1:T(8,128)(2,1)}, bf16[384,1536]{0,1:T(8,128)(2,1)}, u32[]{:S(2)}, u32[]{:S(2)}) collective-permute-start(bf16[384,1536]{0,1:T(8,128)(2,1)} %get-tuple-element.417), channel_id=1, source_target_pairs={{0,1},{1,0},{2,3},{3,2},{4,5},{5,4},{6,7},{7,6},{8,9},{9,8},{10,11... | collective-permute-start | bytes 3538952 | tf_op jit(solution)/shard_map/ppermute | solution.py:500
  (70 other events, 363.2 us)

commit v2 on v1

v2 whole, which is shorter than its diff:
```python
import functools

import jax
import jax.numpy as jnp
from jax import lax
from jax.experimental import pallas as pl
from jax.experimental.pallas import tpu as pltpu
from jax.sharding import PartitionSpec as P

BLK = 256
HD = 64
EPSILON = 1e-05
MESH = pl.DeviceIdType.MESH
f32, bf16 = jnp.float32, jnp.bfloat16

def geometry():
    F, S = lax.axis_size("fsdp"), lax.axis_size("seq")
    return F, S, 4, F // 4, S // 2


class Place:
    def __init__(self):
        self.F, self.S, self.H, self.L, self.X = geometry()
        self.f, self.s = lax.axis_index("fsdp"), lax.axis_index("seq")
        self.h, self.l = self.f // self.L, self.f % self.L
        self.x, self.c = self.s // 2, self.s % 2

    def shard(self, k, j):
        return lax.rem(self.h + self.H - k, self.H) * self.L + lax.rem(self.l + self.L - j, self.L)

    def hi(self, k):
        return (lax.rem(self.h + k, self.H) * self.L + self.l, self.s)

    def lo(self, j):
        return (self.h * self.L + lax.rem(self.l + j, self.L), self.s)

    def across(self, i):
        return (self.f, lax.rem(self.x + i, self.X) * 2 + self.c)

    def sibling(self):
        return (self.f, self.x * 2 + 1 - self.c)

    def everyone(self):
        return (
            [self.hi(k) for k in range(1, self.H)]
            + [self.lo(j) for j in range(1, self.L)]
            + [(self.f, lax.rem(self.s + i, self.S)) for i in range(1, self.S)]
        )


def greet(place):
    barrier = pltpu.get_barrier_semaphore()
    peers = place.everyone()
    for peer in peers:
        pl.semaphore_signal(barrier, inc=1, device_id=peer, device_id_type=MESH)
    pl.semaphore_wait(barrier, len(peers))


def vector(ref, places, name):
    at, size = places[name]
    parts = []
    for f in range(ref.shape[0]):
        pos = at
        while pos < at + size:
            row, lane = divmod(pos, 128)
            count = min(128 - lane, at + size - pos)
            parts.append(ref[f, row : row + 1, lane : lane + count])
            pos += count
    return jnp.concatenate(parts, axis=1)


def normalised(x):
    centre = x - jnp.mean(x, axis=-1, keepdims=True)
    return centre * lax.rsqrt(jnp.mean(centre * centre, axis=-1, keepdims=True) + EPSILON)


def gelu_and_slope(u):
    root = 0.7978845608028654
    square = u * u
    t = jnp.tanh(u * (root + root * 0.044715 * square))
    half = 0.5 * (1.0 + t)
    return u * half, half + u * (0.5 * (1.0 - t * t)) * (root + 3.0 * root * 0.044715 * square)


NT = (((1,), (1,)), ((), ()))
TN = (((0,), (0,)), ((), ()))


def head_lanes(shape, parity):
    lane = lax.broadcasted_iota(jnp.int32, shape, 1)
    return (lane // HD) == parity

def pick(rows, parity):
    return jnp.where(head_lanes(rows.shape, parity), rows, jnp.zeros_like(rows))

def turn(rows):
    return rows.astype(f32).T

def attend_block(i, wide, qkv, vT, scores, oT, lse):
    rows = pl.ds(i * BLK, BLK)
    @pl.loop(0, wide // HD)
    def _(h):
        pair = pl.multiple_of(h // 2 * 128, 128)
        q = pick(qkv[rows, pl.ds(pair, 128)], h % 2) * jnp.asarray(HD ** -0.5, bf16)
        top = jnp.full((8, BLK), -jnp.inf, f32)
        for j in range(i + 1):
            k = qkv[pl.ds(j * BLK, BLK), pl.ds(pl.multiple_of(wide + pair, 128), 128)]
            s = lax.dot_general(k, q, NT, preferred_element_type=f32)
            scores[pl.ds(j * BLK, BLK), :] = s
            top = jnp.maximum(top, jnp.max(s.reshape(BLK // 8, 8, BLK), axis=0))
        top = jnp.max(top, axis=0, keepdims=True)
        total = jnp.zeros((8, BLK), f32)
        out = jnp.zeros((HD, BLK), f32)
        for j in range(i + 1):
            p = jnp.exp(scores[pl.ds(j * BLK, BLK), :] - top)
            total = total + jnp.sum(p.reshape(BLK // 8, 8, BLK), axis=0)
            out = out + jnp.dot(vT[pl.ds(pl.multiple_of(h * HD, HD), HD), pl.ds(j * BLK, BLK)], p.astype(bf16), preferred_element_type=f32)
        total = jnp.sum(total, axis=0, keepdims=True)
        oT[pl.ds(pl.multiple_of(h * HD, HD), HD), :] = out * (1.0 / total)
        lse[pl.ds(h, 1), rows] = top + jnp.log(total)

def attend_back_block(i, wide, qkv, grad, kT, lse, delta, dqT, dk, dv):
    rows = pl.ds(i * BLK, BLK)
    @pl.loop(0, wide // HD)
    def _(h):
        pair = pl.multiple_of(h // 2 * 128, 128)
        here = pl.ds(pair, 128)
        q = pick(qkv[rows, here], h % 2) * jnp.asarray(HD ** -0.5, bf16)
        g = pick(grad[rows, here], h % 2)
        low = lse[pl.ds(h, 1), rows]
        mean = delta[pl.ds(h, 1), rows]
        out = jnp.zeros((HD, BLK), f32)
        for j in range(i + 1):
            keys = pl.ds(j * BLK, BLK)
            k = qkv[keys, pl.ds(pl.multiple_of(wide + pair, 128), 128)]
            v = qkv[keys, pl.ds(pl.multiple_of(2 * wide + pair, 128), 128)]
            p = jnp.exp(lax.dot_general(k, q, NT, preferred_element_type=f32) - low)
            dp = lax.dot_general(v, g, NT, preferred_element_type=f32)
            ds = (p * (dp - mean)).astype(bf16)
            dvj = jnp.dot(p.astype(bf16), g, preferred_element_type=f32)
            dkj = jnp.dot(ds, q, preferred_element_type=f32)
            dv[keys, here] += dvj
            dk[keys, here] += dkj
            out = out + jnp.dot(kT[pl.ds(pl.multiple_of(h * HD, HD), HD), keys], ds, preferred_element_type=f32)
        dqT[pl.ds(pl.multiple_of(h * HD, HD), HD), :] = out * HD ** -0.5


def forward_kernel(places, *refs):
    refs = list(refs)

    def take(count):
        got = refs[:count]
        del refs[:count]
        return got

    tokens, small = take(2)
    shards = take(4)
    big_outs = take(4)
    (small_out, one_out, qkv_out, lse_out, heads_out, mixed_out, middle_out, two_out, act_out,
     slope_out, result_out, stats_out) = take(12)
    wholes = take(4)
    (smalls, smalls_f, one, split, qkv, vT, scores, oT, lse, heads, mixed, middle, two, act, slope,
     result, stats, vectors, wide_bias) = take(19)
    (own_sem, send_sem, save_sem, hi_sem, lo_sem, x_sem, core_sem, sm_hi_sem, sm_lo_sem, there_sem,
     back_sem) = refs
    p = Place()
    S, H, L, X, F = p.S, p.H, p.L, p.X, p.F
    rows_here, D = tokens.shape
    wide = D // S
    sent, saved = [], []

    def push(src, dst, sem, peer):
        cp = pltpu.make_async_remote_copy(
            src_ref=src, dst_ref=dst, send_sem=send_sem.at[0], recv_sem=sem, device_id=peer,
            device_id_type=MESH,
        )
        cp.start()
        sent.append(cp)

    def arrived(dst, sem):
        pltpu.make_async_copy(dst, dst, sem).wait()

    def save(src, dst):
        cp = pltpu.make_async_copy(src, dst, save_sem.at[len(saved)])
        cp.start()
        saved.append(cp)

    own = []
    for w in range(4):
        own.append(pltpu.make_async_copy(shards[w], wholes[w].at[p.f], own_sem.at[w]))
    own.append(pltpu.make_async_copy(small, smalls.at[p.f], own_sem.at[4]))
    for cp in own:
        cp.start()
    greet(p)

    width = 5 - X
    step = 3 // (X - 1) if X > 1 else 0

    def cols(w, start, count):
        C = shards[w].shape[-1]
        return pl.ds(pl.multiple_of(p.c * (C // 2) + start * (C // 8), 128), count * (C // 8))

    def half(w, core):
        C = shards[w].shape[-1]
        return pl.ds(pl.multiple_of(core * (C // 2), 128), C // 2)

    def start_hi(w):
        mine = cols(w, p.x, width)
        for k in range(1, H):
            push(shards[w].at[:, mine], wholes[w].at[p.f, :, mine], hi_sem.at[w, k - 1], p.hi(k))
        for j in range(1, L):
            push(shards[w].at[:, mine], wholes[w].at[p.f, :, mine], lo_sem.at[w, j - 1, 0], p.lo(j))

    def over_x(w, j, k):
        piece = wholes[w].at[p.shard(k, j), :, cols(w, p.x * step, 1)]
        for i in range(1, X):
            push(piece, piece, x_sem.at[w, i - 1, j * H + k - 1], p.across(i))

    def finish_hi(w, k):
        piece = wholes[w].at[p.shard(k, 0), :, cols(w, p.x, width)]
        arrived(piece, hi_sem.at[w, k - 1])
        for j in range(1, L):
            push(piece, piece, lo_sem.at[w, j - 1, k], p.lo(j))
        over_x(w, 0, k)

    def finish_lo(w, k):
        for j in range(1, L):
            arrived(wholes[w].at[p.shard(k, j), :, cols(w, p.x, width)], lo_sem.at[w, j - 1, k])
            over_x(w, j, k)

    def finish_x(w, j, k):
        for i in range(1, X):
            theirs = lax.rem(p.x + X - i, X) * step
            arrived(wholes[w].at[p.shard(k, j), :, cols(w, theirs, 1)], x_sem.at[w, i - 1, j * H + k - 1])
        piece = wholes[w].at[p.shard(k, j), :, half(w, p.c)]
        push(piece, piece, core_sem.at[w, j * H + k - 1], p.sibling())

    def finish_core(w):
        for j in range(L):
            for k in range(H):
                if (j, k) != (0, 0):
                    arrived(wholes[w].at[p.shard(k, j), :, half(w, 1 - p.c)], core_sem.at[w, j * H + k - 1])
        own[w].wait()
        save(wholes[w], big_outs[w])

    def queue_of(w):
        todo = []
        for k in range(1, H):
            todo.append(functools.partial(finish_hi, w, k))
            todo.append(functools.partial(finish_lo, w, k - 1))
        todo.append(functools.partial(finish_lo, w, H - 1))
        for k in range(1, H):
            todo.append(functools.partial(finish_x, w, 0, k))
        for j in range(1, L):
            for k in range(H):
                todo.append(functools.partial(finish_x, w, j, k))
        todo.append(functools.partial(finish_core, w))
        return todo

    def run(todo, count):
        for _ in range(min(count, len(todo))):
            todo.pop(0)()

    for k in range(1, H):
        push(small, smalls.at[p.f], sm_hi_sem.at[k - 1], p.hi(k))
    for j in range(1, L):
        push(small, smalls.at[p.f], sm_lo_sem.at[j - 1, 0], p.lo(j))
    start_hi(0)
    for k in range(1, H):
        piece = smalls.at[p.shard(k, 0)]
        arrived(piece, sm_hi_sem.at[k - 1])
        for j in range(1, L):
            push(piece, piece, sm_lo_sem.at[j - 1, k], p.lo(j))
    for j in range(1, L):
        for k in range(H):
            arrived(smalls.at[p.shard(k, j)], sm_lo_sem.at[j - 1, k])
    own[4].wait()
    smalls_f[...] = smalls[...].astype(f32)
    save(smalls, small_out)
    vec = functools.partial(vector, smalls_f, places)

    chunk = 128
    stats[...] = jnp.zeros_like(stats)
    gain, shift = vec("ln1_gain"), vec("ln1_bias")

    @pl.loop(0, rows_here // chunk)
    def _(t):
        at = pl.ds(pl.multiple_of(t * chunk, chunk), chunk)
        x = tokens[at, :].astype(f32)
        stats[0:1, :] += jnp.sum(x * x, axis=0, keepdims=True)
        one[at, :] = (normalised(x) * gain + shift).astype(bf16)

    save(one, one_out)
    first, second, third, fourth = (queue_of(w) for w in range(4))
    run(first, 1)
    start_hi(1)
    run(first, 4)
    start_hi(2)
    run(first, len(first))

    bias_qv = vec("b_qv")

    def project(kind, target):
        at = pl.multiple_of(kind * D + target * wide, 128)
        w = wholes[0][:, :, pl.ds(at, wide)].reshape(D, wide)
        return jnp.dot(one[...], w, preferred_element_type=f32)

    vectors[0:1, :] = bias_qv[:, :D]
    vectors[1:2, :] = bias_qv[:, D:]

    def heads_of(target):
        lanes = pl.ds(pl.multiple_of(target * wide, 128), wide)
        return [
            (project(0, target) + vectors[0:1, lanes]).astype(bf16),
            project(1, target).astype(bf16),
            (project(2, target) + vectors[1:2, lanes]).astype(bf16),
        ]

    mine = pl.ds(pl.multiple_of(p.s * rows_here, 128), rows_here)
    for i in list(range(1, S)) + [0]:
        target = lax.rem(p.s + i, S)
        for kind, values in enumerate(heads_of(target)):
            if i == 0:
                qkv[mine, kind * wide : (kind + 1) * wide] = values
            else:
                split[i - 1, :, kind * wide : (kind + 1) * wide] = values
        if i:
            push(split.at[i - 1], qkv.at[mine, :], there_sem.at[i - 1], (p.f, target))
    run(second, 7)
    run(third, 1)
    run(second, len(second))
    run(third, 3)
    start_hi(3)
    run(third, 1)
    for i in range(1, S):
        source = lax.rem(p.s + S - i, S)
        arrived(qkv.at[pl.ds(pl.multiple_of(source * rows_here, 128), rows_here), :], there_sem.at[i - 1])
    save(qkv, qkv_out)

    length = qkv.shape[0]
    blocks = length // BLK
    for b in range(blocks):
        at = pl.ds(b * BLK, BLK)
        vT[:, at] = turn(qkv[at, 2 * wide :]).astype(bf16)
    lse[...] = jnp.zeros_like(lse)
    sent_back = 0
    for i in range(blocks):
        attend_block(i, wide, qkv, vT, scores, oT, lse)
        heads[pl.ds(i * BLK, BLK), :] = turn(oT[...]).astype(bf16)
        while (sent_back + 1) * rows_here <= (i + 1) * BLK:
            rows = pl.ds(sent_back * rows_here, rows_here)
            lanes = pl.ds(pl.multiple_of(p.s * wide, 128), wide)

            @pl.when(p.s != sent_back)
            def _():
                pltpu.make_async_remote_copy(
                    src_ref=heads.at[rows], dst_ref=mixed.at[:, lanes], send_sem=send_sem.at[1],
                    recv_sem=back_sem.at[p.s], device_id=(p.f, jnp.int32(sent_back)),
                    device_id_type=MESH,
                ).start()

            @pl.when(p.s == sent_back)
            def _():
                mixed[:, lanes] = heads[rows, :]

            sent_back += 1
        run(third, 2)
    save(heads, heads_out)
    save(lse, lse_out)
    run(third, 3)
    for i in range(1, S):
        source = lax.rem(p.s + S - i, S)
        arrived(mixed.at[:, pl.ds(pl.multiple_of(source * wide, 128), wide)], back_sem.at[source])
    save(mixed, mixed_out)

    tile = 256
    vectors[0:1, :] = vec("b_out")

    @pl.loop(0, D // tile)
    def _(t):
        at = pl.ds(pl.multiple_of(t * tile, tile), tile)
        w = wholes[1][:, :, at].reshape(D, tile)
        branch = jnp.dot(mixed[...], w, preferred_element_type=f32) + vectors[0:1, at]
        middle[:, at] = tokens[:, at].astype(f32) + branch

    save(middle, middle_out)
    gain_two, shift_two = vec("ln2_gain"), vec("ln2_bias")

    @pl.loop(0, rows_here // chunk)
    def _(t):
        at = pl.ds(pl.multiple_of(t * chunk, chunk), chunk)
        x = middle[at, :]
        stats[1:2, :] += jnp.sum(x * x, axis=0, keepdims=True)
        two[at, :] = (normalised(x) * gain_two + shift_two).astype(bf16)

    save(two, two_out)
    run(third, len(third))
    run(fourth, 2)
    wide_bias[0:1, :] = vec("b_fc")

    FF = act.shape[1]

    @pl.loop(0, FF // tile)
    def _(t):
        at = pl.ds(pl.multiple_of(t * tile, tile), tile)
        w = wholes[2][:, :, at].reshape(D, tile)
        u = jnp.dot(two[...], w, preferred_element_type=f32) + wide_bias[0:1, at]
        act_rows, slope_rows = gelu_and_slope(u)
        act[:, at] = act_rows.astype(bf16)
        slope[:, at] = slope_rows.astype(bf16)

    save(act, act_out)
    save(slope, slope_out)
    run(fourth, len(fourth))
    vectors[0:1, :] = vec("b_proj")

    @pl.loop(0, D // tile)
    def _(t):
        at = pl.ds(pl.multiple_of(t * tile, tile), tile)
        w = wholes[3][:, :, at].reshape(FF, tile)
        stream = middle[:, at] + (jnp.dot(act[...], w, preferred_element_type=f32) + vectors[0:1, at])
        stats[2:3, at] = jnp.sum(stream * stream, axis=0, keepdims=True)
        result[:, at] = stream.astype(bf16)

    save(result, result_out)
    save(stats, stats_out)
    for cp in sent:
        cp.wait_send()
    for i in range(1, S):
        arrived(heads.at[pl.ds(0, rows_here)], send_sem.at[1])
    for cp in saved:
        cp.wait()


def forward(tokens, packed, places, shards):
    F, S, H, L, X = geometry()
    rows_here, D = tokens.shape
    wide, length, FF = D // S, rows_here * S, shards[2].shape[1]
    heads = max(8, wide // HD)
    lead = max(X - 1, 1)
    any_spec = pl.BlockSpec(memory_space=pl.ANY)
    V, D_SEM = pltpu.VMEM, pltpu.SemaphoreType.DMA
    shaped = jax.ShapeDtypeStruct
    wholes = [(F,) + a.shape for a in shards]
    outs = [shaped(s, bf16) for s in wholes] + [
        shaped((F,) + packed.shape, bf16),
        shaped((rows_here, D), bf16),
        shaped((length, 3 * wide), bf16),
        shaped((heads, length), f32),
        shaped((length, wide), bf16),
        shaped((rows_here, D), bf16),
        shaped((rows_here, D), f32),
        shaped((rows_here, D), bf16),
        shaped((rows_here, FF), bf16),
        shaped((rows_here, FF), bf16),
        shaped((rows_here, D), bf16),
        shaped((8, D), f32),
    ]
    return pl.pallas_call(
        functools.partial(forward_kernel, places),
        out_shape=outs,
        in_specs=[pl.BlockSpec(memory_space=pltpu.VMEM)] + [any_spec] * 5,
        out_specs=[any_spec] * len(outs),
        scratch_shapes=[V(s, bf16) for s in wholes]
        + [
            V((F,) + packed.shape, bf16),
            V((F,) + packed.shape, f32),
            V((rows_here, D), bf16),
            V((S - 1, rows_here, 3 * wide), bf16),
            V((length, 3 * wide), bf16),
            V((wide, length), bf16),
            V((length, BLK), f32),
            V((wide, BLK), f32),
            V((heads, length), f32),
            V((length, wide), bf16),
            V((rows_here, D), bf16),
            V((rows_here, D), f32),
            V((rows_here, D), bf16),
            V((rows_here, FF), bf16),
            V((rows_here, FF), bf16),
            V((rows_here, D), bf16),
            V((8, D), f32),
            V((8, D), f32),
            V((8, FF), f32),
            D_SEM((5,)),
            D_SEM((2,)),
            D_SEM((len(outs),)),
            D_SEM((4, H - 1)),
            D_SEM((4, L - 1, H)),
            D_SEM((4, lead, F - 1)),
            D_SEM((4, F - 1)),
            D_SEM((H - 1,)),
            D_SEM((L - 1, H)),
            D_SEM((S - 1,)),
            D_SEM((S,)),
        ],
        compiler_params=pltpu.CompilerParams(
            collective_id=1, has_side_effects=True, vmem_limit_bytes=60 * 2**20
        ),
    )(tokens, packed, *shards)


def rs_kernel(n, *refs):
    given, small = refs[:n], refs[n]
    outs, small_out = refs[n + 1:2 * n + 1], refs[2 * n + 1]
    rest = list(refs[2 * n + 2:])
    def take(k):
        got = rest[:k]; del rest[:k]; return got
    parts, from_x, from_lo, from_hi, value, from_x_end, half_out = (take(n) for _ in range(7))
    sm_core, sm_x, sm_sum, sm_lo, sm_hi = take(5)
    load_sem, send_sem, x_sem, lo_sem, hi_sem, end_sem, out_sem, core_sem, sm_sem, smx_sem, smlo_sem, smhi_sem = rest
    loads = [pltpu.make_async_copy(given[w], parts[w], load_sem.at[w]) for w in range(n)]
    for load in loads: load.start()
    p = Place()
    greet(p)
    H, L, X = p.H, p.L, p.X
    width = 5 - X
    step = 3 // (X - 1) if X > 1 else 0
    sent = []
    def push(src, dst, sem, peer):
        cp = pltpu.make_async_remote_copy(src_ref=src, dst_ref=dst, send_sem=send_sem.at[0], recv_sem=sem, device_id=peer, device_id_type=MESH)
        cp.start(); sent.append(cp)
    def arrived(dst, sem):
        pltpu.make_async_copy(dst, dst, sem).wait()
    def unit(w): return parts[w].shape[-1] // 4
    def span(w, start, count):
        return pl.ds(pl.multiple_of(start * unit(w), 128), count * unit(w))
    def other_x(i): return lax.rem(p.x + i, X)
    def shard(k, j):
        return lax.rem(p.h + k, H) * L + lax.rem(p.l + j, L)
    def s1(w):
        loads[w].wait()
        for j in list(range(1, L)) + [0]:
            for k in range(H):
                for i in range(1, X):
                    f = shard(k, j)
                    push(parts[w].at[f, :, span(w, other_x(i) * step, 1)], from_x[w].at[i - 1, f], x_sem.at[w, i - 1, j * H + k], p.across(i))
    def add_x(w, k, j):
        f = shard(k, j)
        for i in range(1, X):
            arrived(from_x[w].at[i - 1, f], x_sem.at[w, i - 1, j * H + k])
        if X > 1:
            cols = span(w, p.x * step, 1)
            total = parts[w][f, :, cols].astype(f32)
            for i in range(1, X):
                total = total + from_x[w][i - 1, f].astype(f32)
            parts[w][f, :, cols] = total.astype(bf16)
    def s2(w):
        for j in range(1, L):
            for k in list(range(1, H)) + [0]:
                add_x(w, k, j)
                f = shard(k, j)
                push(parts[w].at[f, :, span(w, p.x, width)], from_lo[w].at[j - 1, lax.rem(p.h + k, H)], lo_sem.at[w, j - 1, k], p.lo(j))
    def s3(w):
        for k in list(range(1, H)) + [0]:
            add_x(w, k, 0)
            h = lax.rem(p.h + k, H)
            f = h * L + p.l
            cols = span(w, p.x, width)
            total = parts[w][f, :, cols].astype(f32)
            for j in range(1, L):
                arrived(from_lo[w].at[j - 1, h], lo_sem.at[w, j - 1, k])
                total = total + from_lo[w][j - 1, h].astype(f32)
            parts[w][f, :, cols] = total.astype(bf16)
            if k > 0:
                push(parts[w].at[f, :, cols], from_hi[w].at[k - 1], hi_sem.at[w, k - 1], p.hi(k))
    def s4(w):
        cols = span(w, p.x, width)
        total = parts[w][p.f, :, cols].astype(f32)
        for k in range(1, H):
            arrived(from_hi[w].at[k - 1], hi_sem.at[w, k - 1])
            total = total + from_hi[w][k - 1].astype(f32)
        value[w][:, cols] = total.astype(bf16)
        for i in range(1, X):
            push(value[w].at[:, cols], from_x_end[w].at[i - 1, :, cols], end_sem.at[w, i - 1], p.across(i))
    def s5(w):
        mine = span(w, p.x * step, 1)
        half_out[w][:, mine] = value[w][:, mine].astype(f32)
        for i in range(1, X):
            src = lax.rem(p.x + X - i, X)
            cols = span(w, src, width)
            arrived(from_x_end[w].at[i - 1, :, cols], end_sem.at[w, i - 1])
            theirs = span(w, src * step, 1)
            half_out[w][:, theirs] = from_x_end[w][i - 1, :, theirs].astype(f32)
        if X < 4:
            both = pl.ds(unit(w), (4 - X) * unit(w))
            total = value[w][:, both].astype(f32)
            for i in range(1, X):
                total = total + from_x_end[w][i - 1, :, both].astype(f32)
            half_out[w][:, both] = total
        there = outs[w].at[:, pl.ds(pl.multiple_of(p.c * 4 * unit(w), 128), 4 * unit(w))]
        push(half_out[w], there, core_sem.at[w], p.sibling())
        pltpu.make_async_copy(half_out[w], there, out_sem.at[w]).start()
    def s6(w):
        arrived(half_out[w], core_sem.at[w])
        arrived(half_out[w], out_sem.at[w])
    def t0():
        push(small, sm_core, sm_sem.at[0], p.sibling())
    def t1():
        arrived(sm_core, sm_sem.at[0])
        sm_x[p.x] = small[...] + sm_core[...]
        for i in range(1, X):
            push(sm_x.at[p.x], sm_x.at[p.x], smx_sem.at[i - 1], p.across(i))
    def t2():
        for i in range(1, X):
            arrived(sm_x.at[lax.rem(p.x + X - i, X)], smx_sem.at[i - 1])
        total = sm_x[0]
        for i in range(1, X): total = total + sm_x[i]
        sm_sum[...] = total
        for j in range(1, L):
            for k in range(H):
                h = lax.rem(p.h + k, H)
                push(sm_sum.at[shard(k, j)], sm_lo.at[j - 1, h], smlo_sem.at[j - 1, k], p.lo(j))
    def t3():
        for k in range(H):
            h = lax.rem(p.h + k, H)
            f = h * L + p.l
            total = sm_sum[f]
            for j in range(1, L):
                arrived(sm_lo.at[j - 1, h], smlo_sem.at[j - 1, k])
                total = total + sm_lo[j - 1, h]
            sm_core[f] = total
            if k > 0:
                push(sm_core.at[f], sm_hi.at[k - 1], smhi_sem.at[k - 1], p.hi(k))
    def t4():
        total = sm_core[p.f]
        for k in range(1, H):
            arrived(sm_hi.at[k - 1], smhi_sem.at[k - 1])
            total = total + sm_hi[k - 1]
        small_out[...] = total
    s1(0)
    stages = [s2, s3, s4, s5]
    for t in range(n + 3):
        for d, stage in enumerate(stages):
            if 0 <= t - d < n: stage(t - d)
            if d == 0 and t + 1 < n: s1(t + 1)
        if t == 0: t0()
        if t == 1: t1()
        if t == 2: t2()
        if t == 3: t3()
        if t == 4: t4()
    for w in range(n): s6(w)
    for cp in sent: cp.wait_send()

def reduce_all(parts, small):
    F, S, H, L, X = geometry()
    n = len(parts)
    width = 5 - X
    V = pltpu.VMEM
    def each(shape_of, dt):
        return [V(shape_of(a.shape[1], a.shape[2] // 4), dt) for a in parts]
    D = pltpu.SemaphoreType.DMA
    lead = max(X - 1, 1)
    res = pl.pallas_call(
        functools.partial(rs_kernel, n),
        out_shape=[jax.ShapeDtypeStruct((a.shape[1], 2 * a.shape[2]), f32) for a in parts] + [jax.ShapeDtypeStruct(small.shape[1:], f32)],
        in_specs=[pl.BlockSpec(memory_space=pl.ANY)] * n + [pl.BlockSpec(memory_space=pltpu.VMEM)],
        out_specs=[pl.BlockSpec(memory_space=pl.ANY)] * n + [pl.BlockSpec(memory_space=pltpu.VMEM)],
        scratch_shapes=[V(a.shape, bf16) for a in parts] + each(lambda r, u: (lead, F, r, u), bf16) + each(lambda r, u: (L - 1, H, r, width * u), bf16)
          + each(lambda r, u: (H - 1, r, width * u), bf16) + each(lambda r, u: (r, 4 * u), bf16) + each(lambda r, u: (lead, r, 4 * u), bf16)
          + each(lambda r, u: (r, 4 * u), f32)
          + [V(small.shape, f32), V((X,) + small.shape, f32), V(small.shape, f32), V((L - 1, H) + small.shape[1:], f32), V((H - 1,) + small.shape[1:], f32)]
          + [D((n,)), D((1,)), D((n, lead, F)), D((n, L - 1, H)), D((n, H - 1)), D((n, lead)), D((n,)), D((n,)), D((1,)), D((lead,)), D((L - 1, H)), D((H - 1,))],
        compiler_params=pltpu.CompilerParams(collective_id=2, has_side_effects=True, vmem_limit_bytes=60 * 2**20),
    )(*parts, small)
    return res[:n], res[n]


def attention_back(qkv, grad, heads_out, lse):
    length, wide = grad.shape

    def kernel(qkv, grad, mixed, lse, out, kT, delta, dqT, dk, dv):
        dk[...] = jnp.zeros_like(dk)
        dv[...] = jnp.zeros_like(dv)
        shape = (lse.shape[0], wide)
        chosen = lax.broadcasted_iota(jnp.int32, shape, 1) // HD == lax.broadcasted_iota(jnp.int32, shape, 0)
        chosen = jnp.where(chosen, 1.0, 0.0).astype(bf16)
        for b in range(length // BLK):
            at = pl.ds(b * BLK, BLK)
            kT[:, at] = turn(qkv[at, wide : 2 * wide]).astype(bf16)
            product = grad[at, :].astype(f32) * mixed[at, :].astype(f32)
            high = product.astype(bf16)
            low = (product - high.astype(f32)).astype(bf16)
            delta[:, at] = lax.dot_general(chosen, high, NT, preferred_element_type=f32) + lax.dot_general(
                chosen, low, NT, preferred_element_type=f32
            )
        for i in range(length // BLK):
            attend_back_block(i, wide, qkv, grad, kT, lse, delta, dqT, dk, dv)
            out[i * BLK : (i + 1) * BLK, 0:wide] = turn(dqT[...]).astype(bf16)
        out[:, wide : 2 * wide] = dk[...].astype(bf16)
        out[:, 2 * wide :] = dv[...].astype(bf16)

    V = pltpu.VMEM
    return pl.pallas_call(
        kernel,
        out_shape=jax.ShapeDtypeStruct((length, 3 * wide), bf16),
        scratch_shapes=[
            V((wide, length), bf16), V(lse.shape, f32), V((wide, BLK), f32), V((length, wide), f32),
            V((length, wide), f32),
        ],
        compiler_params=pltpu.CompilerParams(vmem_limit_bytes=48 * 2**20),
    )(qkv, grad, heads_out, lse)


def layer_norm(values, gain_vec, shift):
    centre = values - jnp.mean(values, axis=-1, keepdims=True)
    spread = jnp.mean(centre * centre, axis=-1, keepdims=True)
    return centre * lax.rsqrt(spread + EPSILON) * gain_vec + shift


def on_device(
    tokens, cotangent, ln1_gain, ln1_bias, w_qkv, b_qv, w_out, b_out,
    ln2_gain, ln2_bias, w_fc, b_fc, w_proj, b_proj,
):
    F, S, H, L, X = geometry()
    row_count, D = tokens.shape
    named = dict(
        b_fc=b_fc, b_qv=b_qv, ln1_gain=ln1_gain, ln1_bias=ln1_bias, b_out=b_out,
        ln2_gain=ln2_gain, ln2_bias=ln2_bias, b_proj=b_proj,
    )
    places, at = {}, 0
    for name, value in named.items():
        places[name] = (at, value.shape[0])
        at += value.shape[0]
    flat = jnp.concatenate(list(named.values()))
    small_rows = -(-at // 2048) * 16
    flat = jnp.pad(flat, (0, small_rows * 128 - at)).reshape(small_rows, 128)
    (weight_qkv, weight_out, weight_fc, weight_proj, smalls, normed_one, qkv, lse, heads_out,
     mixed_tokens, middle, normed_two, activated, slope, output, stats) = forward(
        tokens, flat, places, [w_qkv, w_out, w_fc, w_proj]
    )
    weight_qkv, weight_out, weight_fc, weight_proj = (
        a.reshape(-1, a.shape[-1]) for a in (weight_qkv, weight_out, weight_fc, weight_proj)
    )
    smalls = smalls.reshape(F, -1).astype(f32)
    whole = {n: smalls[:, a : a + size].reshape(-1) for n, (a, size) in places.items()}
    cell_count = row_count * D * S * F
    inputs = tokens.astype(f32)
    grad_out = cotangent.astype(f32)
    grads = dict(b_proj=jnp.sum(grad_out, axis=0))
    grad_act = jnp.einsum("td,fd->tf", cotangent, weight_proj, preferred_element_type=f32)
    grad_before = (slope.astype(f32) * grad_act).astype(bf16)
    grads["b_fc"] = jnp.sum(grad_before, axis=0, dtype=f32)
    grad_normed_two = jnp.einsum("tf,df->td", grad_before, weight_fc, preferred_element_type=f32)
    _, pull_two = jax.vjp(layer_norm, middle, whole["ln2_gain"], whole["ln2_bias"])
    grad_mid_norm, grads["ln2_gain"], grads["ln2_bias"] = pull_two(grad_normed_two)
    grad_middle = grad_out + grad_mid_norm
    grad_branch = grad_middle.astype(bf16)
    grads["b_out"] = jnp.sum(grad_branch, axis=0, dtype=f32)
    grad_mixed = jnp.einsum(
        "td,id->ti", grad_branch, weight_out, preferred_element_type=f32
    ).astype(bf16)
    grad_heads = lax.all_to_all(grad_mixed, "seq", split_axis=1, concat_axis=0, tiled=True)
    grad_qkv = attention_back(qkv, grad_heads, heads_out, lse)
    grad_projected = lax.all_to_all(
        grad_qkv.reshape(-1, 3, D // S), "seq", split_axis=0, concat_axis=2, tiled=True
    ).reshape(row_count, 3 * D)
    grads["b_qv"] = jnp.concatenate(
        [
            jnp.sum(grad_projected[:, :D], axis=0, dtype=f32),
            jnp.sum(grad_projected[:, 2 * D :], axis=0, dtype=f32),
        ]
    )
    grad_normed_one = jnp.einsum(
        "te,de->td", grad_projected, weight_qkv, preferred_element_type=f32
    )
    _, pull_one = jax.vjp(layer_norm, inputs, whole["ln1_gain"], whole["ln1_bias"])
    grad_in_norm, grads["ln1_gain"], grads["ln1_bias"] = pull_one(grad_normed_one)
    grad_tokens = (grad_middle + grad_in_norm).astype(bf16)

    core = lax.axis_index("seq") % 2
    pairs = [(s, s + 1 - 2 * (s % 2)) for s in range(S)]

    def half_grad(rows, columns):
        wide = columns.shape[1] // 2
        mine = lax.dynamic_slice_in_dim(columns, core * wide, wide, 1)
        theirs = lax.dynamic_slice_in_dim(columns, (1 - core) * wide, wide, 1)
        both_rows = jnp.concatenate([rows, lax.ppermute(rows, "seq", pairs)], axis=0)
        both_columns = jnp.concatenate([mine, lax.ppermute(theirs, "seq", pairs)], axis=0)
        grad = jnp.einsum("ta,tb->ab", both_rows, both_columns, preferred_element_type=f32)
        return grad.astype(bf16).reshape(F, -1, wide)

    halves = [
        half_grad(activated, cotangent),
        half_grad(normed_two, grad_before),
        half_grad(mixed_tokens, grad_branch),
        half_grad(normed_one, grad_projected),
    ]
    sums = jnp.sum(stats[:3], axis=1)
    width = at + 3
    total_rows = -(-width // 1024) * 8
    small_grads = jnp.concatenate(
        [grads[name].reshape(F, -1) for name in places]
        + [jnp.broadcast_to(sums, (F, 3)), jnp.zeros((F, total_rows * 128 - width), f32)],
        axis=1,
    ).reshape(F, total_rows, 128)
    (grad_w_proj, grad_w_fc, grad_w_out, grad_w_qkv), reduced = reduce_all(halves, small_grads)
    reduced = reduced.reshape(-1)
    got = {name: reduced[a : a + size] for name, (a, size) in places.items()}
    rms_values = jnp.sqrt(reduced[at : at + 3] / float(cell_count))
    return (
        output, grad_tokens, got["ln1_gain"], got["ln1_bias"], grad_w_qkv, got["b_qv"],
        grad_w_out, got["b_out"], got["ln2_gain"], got["ln2_bias"], grad_w_fc, got["b_fc"],
        grad_w_proj, got["b_proj"], rms_values,
    )


def solution(mesh):
    in_specs = (
        P(("fsdp", "seq"), None),
        P(("fsdp", "seq"), None),
        P("fsdp"),
        P("fsdp"),
        P("fsdp", None),
        P("fsdp"),
        P("fsdp", None),
        P("fsdp"),
        P("fsdp"),
        P("fsdp"),
        P("fsdp", None),
        P("fsdp"),
        P("fsdp", None),
        P("fsdp"),
    )
    out_specs = (
        P(("fsdp", "seq"), None),
        P(("fsdp", "seq"), None),
        P("fsdp"),
        P("fsdp"),
        P("fsdp", None),
        P("fsdp"),
        P("fsdp", None),
        P("fsdp"),
        P("fsdp"),
        P("fsdp"),
        P("fsdp", None),
        P("fsdp"),
        P("fsdp", None),
        P("fsdp"),
        P(),
    )
    return jax.shard_map(
        on_device, mesh=mesh, in_specs=in_specs, out_specs=out_specs, check_vma=False
    )
```

time: 721 us -> 507 us (0.70)
  matrix products: 186 us -> 46.9 us
  Pallas kernels: 293 us -> 356 us
  waiting for transfers between devices: 67.2 us -> 27.9 us
  local copies, waits for them, and re-layouts: 82.5 us -> 44.9 us
  other arithmetic: 46 us -> 10.8 us
  loops' own time: 14.3 us -> 0 us
  starting transfers between devices: 23.1 us -> 12.7 us
    dot_general x25 -> x0, matrix products: 140 us -> none  [the longest x6 33.6 us: block_scores(): jnp.einsum('qhd,khd->hqk', query_rows, keys_all, preferred_element_type=j...]
    pallas_call x1 -> x2, Pallas kernels: 133 us -> 197 us  [the longest x1 171 us: forward(): pl.pallas_call(functools.partial(forward_kernel, places), out_shape=outs,...]
    all_to_all x3 -> x1, waiting for transfers between devices: 62.3 us -> 19.2 us  [on_device(): lax.all_to_all(grad_qkv.reshape(-1, 3, D // S), 'seq', split_axis=0, conc...]
    convert_element_type x5 -> x0, other arithmetic: 14.4 us -> none  [the longest x3 13.7 us: one_block(): grad_scores = (soft_probs * (grad_probs - inner_sum)).astype(jnp.bfloat16)]
    another operation x2 -> x0, loops' own time: 14.3 us -> none  [the longest x1 8.36 us: attend_backward(): lax.scan(one_block, (zero_keys, zero_keys), block_ids)]
    while x85 -> x0, local copies, waits for them, and re-layouts: 10.9 us -> none
    all_to_all x6 -> x2, local copies, waits for them, and re-layouts: 16.9 us -> 6.73 us  [on_device(): lax.all_to_all(grad_qkv.reshape(-1, 3, D // S), 'seq', split_axis=0, conc...]
    reduce_sum x5 -> x3, other arithmetic: 13.7 us -> 3.8 us  [the longest x1 2.26 us: on_device(): grads = dict(b_proj=jnp.sum(grad_out, axis=0))]
  transfers between devices with their start and end apart: 12 -> 10, of which waited for: 4 -> 4; matrix products, arithmetic and copies ran while one was open for 24% -> 11% of each run, Pallas kernels for 0% -> 5%
where the time goes in v2:
time: 507 us; the launch traced here: 500 us
  Pallas kernels  356 us (70%)
  matrix products  46.9 us (9%)
  local copies, waits for them, and re-layouts  44.9 us (9%)
  waiting for transfers between devices  27.9 us (6%)
  starting transfers between devices  12.7 us (3%)
  other arithmetic  10.8 us (2%)
    pallas_call x1, Pallas kernels, forward(): pl.pallas_call(functools.partial(forward_kernel, places), out_shape=outs,...  171 us
    pallas_call x1, Pallas kernels, reduce_all(): pl.pallas_call(functools.partial(rs_kernel, n), out_shape=[jax.ShapeDtype...  159 us
    pallas_call x1, Pallas kernels, attention_back(): pl.pallas_call(kernel, out_shape=jax.ShapeDtypeStruct((length, 3 * wide),...  26.8 us
    dot_general x4, matrix products, half_grad(): jnp.einsum('ta,tb->ab', both_rows, both_columns, preferred_element_type=f32)  25.1 us
    all_to_all x1, waiting for transfers between devices, on_device(): lax.all_to_all(grad_qkv.reshape(-1, 3, D // S), 'seq', split_axis=0, conc...  19.2 us
    unnamed x86, local copies, waits for them, and re-layouts  16.6 us
    dot_general x1, matrix products, on_device(): jnp.einsum('td,fd->tf', cotangent, weight_proj, preferred_element_type=f32)  10.5 us
  transfers between devices with their start and end apart: 10, of which 4 were waited for; matrix products, arithmetic and copies ran while one was open for 11% of the time, Pallas kernels for 5%

profile of v2, /device:TPU:9, one launch (start us, length us, event | category | flops | bytes accessed | tf_op | source)
XLA Modules:
  0.0 500.3 jit_solution(10415149032960143220)
XLA Ops:
  7.9 170.5 %shard_map.253 = (bf16[8,128,3072]{2,1,0:T(8,128)(2,1)}, bf16[8,128,1024]{2,1,0:T(8,128)(2,1)}, bf16[8,128,4096]{2,1,0:T(8,128)(2,1)}, bf16[8,512,1024]{2,1,0:T(...) custom-call(bf16[384,1024]{1,0:T(8,128)(2,1)} %refs_0_.1, ...), custom_call_target="tpu_custom_call" | custom-call | tf_op jit(solution)/shard_map/pallas_call | solution.py:459
  180.0 1.6 reduce_sum.156
  182.0 10.5 %convert_reduce_fusion = (f32[4096]{0:T(1024)}, bf16[384,4096]{1,0:T(8,128)(2,1)S(1)}) fusion(bf16[4096,1024]{1,0:T(8,128)(2,1)} %bitcast.94, bf16[384,1024]{1,0:T(8,128)(2,1)S(1)} %copy-done.6, bf16[384,4096]{1,0:T(8,128)(2,1)} %get-tuple-element.37), kind=kOutput, calls=%fused_computation.6 | convolution fusion | flops 3229085696 | bytes 15482880 | tf_op jit(solution)/shard_map/td,fd->tf/dot_general | solution.py:741
  192.5 4.3 multiply_reduce_fusion
  201.7 3.9 all-to-all-start
  205.7 4.0 constant_dynamic-slice_fusion.5
  209.6 6.5 %all-to-all-done = bf16[384,4,256]{2,0,1:T(8,128)(2,1)S(1)} async-done(((bf16[384,4,256]{2,0,1:T(8,128)(2,1)}), bf16[384,4,256]{2,0,1:T(8,128)(2,1)S(1)}, u32[]{:S(2)}, u32[]{:S(2)}) %all-to-all-start) | async-done | bytes 786464 | tf_op jit(solution)/shard_map/all_to_all | solution.py:753
  217.3 26.8 %shard_map.254 = bf16[1536,768]{1,0:T(8,128)(2,1)S(1)} custom-call(bf16[1536,768]{1,0:T(8,128)(2,1)} %get-tuple-element.42.qkv, bf16[1536,256]{1,0:T(8,128)(2,1)S(1)} %bitcast.70, bf16[1536,256]{1,0:T(8,128)(2,1)S(1)} %copy-done, f32[8,1536]{1,0:T(8,128)S(1)} %copy-done.1), custom_call_target="tpu_custom_call" | custom-call | tf_op jit(solution)/shard_map/pallas_call | solution.py:694
  244.1 2.5 copy.37
  246.6 5.7 %copy.38 = bf16[1536,3,256]{2,1,0:T(4,128)(2,1)} copy(bf16[1536,3,256]{0,2,1:T(8,128)(2,1)} %bitcast.74) | data formatting | bytes 4718592 | tf_op jit(solution)/shard_map/reshape | solution.py:756
  252.2 6.3 %all-to-all-start.1 = ((bf16[1536,3,256]{2,1,0:T(4,128)(2,1)}), bf16[1536,3,256]{2,1,0:T(4,128)(2,1)}, u32[]{:S(2)}, u32[]{:S(2)}) async-start(bf16[1536,3,256]{2,1,0:T(4,128)(2,1)} %copy.38), calls=%async_computation.1 | async-start | bytes 6291456 | tf_op jit(solution)/shard_map/all_to_all | solution.py:755
  263.1 3.5 fusion.32
  266.6 1.4 collective-permute-done.2
  268.0 7.3 %convolution_convert_fusion.1 = bf16[1024,2048]{1,0:T(8,128)(2,1)} fusion(bf16[384,2048]{1,0:T(8,128)(2,1)} %collective-permute-done.3, bf16[384,2048]{1,0:T(8,128)(2,1)S(1)} %copy-done.15, bf16[384,1024]{1,0:T(8,128)(2,1)} %collective-permute-done.2, bf16[384,1024]{1,0:T(8,128)(2,1)} %get-tuple-element.48), kind=kOutput, calls=%fused_computation.9 | convolution fusion | flops 3232759808 | bytes 8912896 | tf_op jit(solution)/shard_map/ta,tb->ab/dot_general | solution.py:780
  275.4 19.2 %all-to-all-done.1 = bf16[1536,3,256]{2,1,0:T(4,128)(2,1)} async-done(((bf16[1536,3,256]{2,1,0:T(4,128)(2,1)}), bf16[1536,3,256]{2,1,0:T(4,128)(2,1)}, u32[]{:S(2)}, u32[]{:S(2)}) %all-to-all-start.1) | async-done | bytes 2359328 | tf_op jit(solution)/shard_map/all_to_all | solution.py:755
  294.6 3.7 copy.39
  298.3 3.0 copy.40
  301.4 1.6 constant_dynamic-slice_fusion.1
  303.9 5.9 %fusion.50 = (f32[1024]{0:T(1024)}, f32[384]{0:T(512)S(1)}, f32[384]{0:T(512)S(1)}, f32[384,1024]{1,0:T(8,128)S(1)}) fusion(f32[1024]{0:T(1024)S(1)} %copy-done.19, f32[384]{0:T(512)S(1)} %copy-done.20, bf16[384,1024]{1,0:T(8,128)(2,1)S(1)} %copy-done.5, bf16[384,3072]{0,1:T(8,128)(2,1)S(1)} %bitcast.72, bf16[1024,3072]{1,0:T(8,128)(2,1)} %bitcast.95), kind=kOutput, calls=%fused_computation.98 | convolution fusion | flops 2419062784 | bytes 11022848 | tf_op jit(solution)/shard_map/te,de->td/dot_general | solution.py:764
  311.4 2.3 convert_reduce_fusion.2
  315.2 8.4 %fusion.5 = bf16[4096,512]{1,0:T(8,128)(2,1)} fusion(bf16[384,4096]{1,0:T(8,128)(2,1)} %collective-permute-done, bf16[384,4096]{1,0:T(8,128)(2,1)} %get-tuple-element.47, bf16[384,512]{1,0:T(8,128)(2,1)} %collective-permute-done.1, bf16[384,512]{1,0:T(8,128)(2,1)S(1)} %get-tuple-element.79), kind=kOutput, calls=%fused_computation.7 | convolution fusion | flops 3237478400 | bytes 11272192 | tf_op jit(solution)/shard_map/ta,tb->ab/dot_general | solution.py:780
  323.7 5.9 %convolution_convert_fusion = bf16[1024,1536]{1,0:T(8,128)(2,1)} fusion(bf16[384,1536]{0,1:T(8,128)(2,1)} %collective-permute-done.7, bf16[384,1536]{0,1:T(8,128)(2,1)S(1)} %copy-done.16, bf16[384,1024]{1,0:T(8,128)(2,1)} %collective-permute-done.6, bf16[384,1024]{1,0:T(8,128)(2,1)S(1)} %copy-done.33), kind=kOutput, calls=%fused_computation.8 | convolution fusion | flops 2425356288 | bytes 7077888 | tf_op jit(solution)/shard_map/ta,tb->ab/dot_general | solution.py:780
  329.5 158.6 %shard_map.255 = (f32[512,1024]{1,0:T(8,128)}, f32[128,4096]{1,0:T(8,128)}, f32[128,1024]{1,0:T(8,128)}, f32[128,3072]{1,0:T(8,128)}, f32[16,128]{1,0:T(8,128)}) custom-call(bf16[8,512,512]{2,1,0:T(8,128)(2,1)} %bitcast.77, bf16[8,128,2048]{2,1,0:T(8,128)(2,1)} %bitcast.76, bf16[8,128,512]{2,1,0:T(8,128)(2,1)} %bitcast.79, bf16[8,128,1536]{2,1,0:T(8,128)(2,1)} %bitcast.78, ...), custom_call_target="tpu_custom_call" | custom-call | tf_op jit(solution)/shard_map/pallas_call | solution.py:654
  488.2 1.4 slice_bitcast_fusion.4
  (135 shorter events, 34.2 us)
Async XLA Ops:
  178.5 3.2 copy-start.2
  181.6 10.8 %slice-start = ((s8[8388608]{0:T(1024)(128)(4,1)}), s8[4194304]{0:T(1024)(128)(4,1)S(1)}, s32[]{:S(2)}) async-start(s8[8388608]{0:T(1024)(128)(4,1)} %bitcast.91), calls=%async_computation.2 | async-start | bytes 8388608
  182.0 10.5 %slice-start.1 = ((s8[8388608]{0:T(1024)(128)(4,1)}), s8[4194304]{0:T(1024)(128)(4,1)S(1)}, s32[]{:S(2)}) async-start(s8[8388608]{0:T(1024)(128)(4,1)} %bitcast.91), calls=%async_computation.3 | async-start | bytes 8388608
  192.5 4.3 copy-start.9
  201.7 14.5 %all-to-all-start = ((bf16[384,4,256]{2,0,1:T(8,128)(2,1)}), bf16[384,4,256]{2,0,1:T(8,128)(2,1)S(1)}, u32[]{:S(2)}, u32[]{:S(2)}) async-start(bf16[384,4,256]{2,0,1:T(8,128)(2,1)} %bitcast.67), calls=%async_computation | async-start | bytes 1572864 | tf_op jit(solution)/shard_map/all_to_all | solution.py:753
  205.6 10.5 %copy-start.1 = (f32[8,1536]{1,0:T(8,128)S(1)}, f32[8,1536]{1,0:T(8,128)}, u32[]{:S(2)}) copy-start(f32[8,1536]{1,0:T(8,128)} %get-tuple-element.45.lse) | copy-start | bytes 147460
  209.6 58.4 %collective-permute-start.3 = (bf16[384,2048]{1,0:T(8,128)(2,1)}, bf16[384,2048]{1,0:T(8,128)(2,1)}, u32[]{:S(2)}, u32[]{:S(2)}) collective-permute-start(bf16[384,2048]{1,0:T(8,128)(2,1)} %get-tuple-element.72), channel_id=1, source_target_pairs={{0,1},{1,0},{2,3},{3,2},{4,5},{5,4},{6,7},{7,6},{8,9},{9,8},{10,11... | collective-permute-start | bytes 4718600 | tf_op jit(solution)/shard_map/ppermute | solution.py:779
  252.2 6.9 %copy-start.11 = (bf16[384,1024]{1,0:T(8,128)(2,1)S(1)}, bf16[384,1024]{1,0:T(8,128)(2,1)}, u32[]{:S(2)}) copy-start(bf16[384,1024]{1,0:T(8,128)(2,1)} %copy-done.10) | copy-start | bytes 2359300
  252.2 42.4 %all-to-all-start.1 = ((bf16[1536,3,256]{2,1,0:T(4,128)(2,1)}), bf16[1536,3,256]{2,1,0:T(4,128)(2,1)}, u32[]{:S(2)}, u32[]{:S(2)}) async-start(bf16[1536,3,256]{2,1,0:T(4,128)(2,1)} %copy.38), calls=%async_computation.1 | async-start | bytes 6291456 | tf_op jit(solution)/shard_map/all_to_all | solution.py:755
  258.5 4.5 collective-permute-start.4
  258.6 56.6 %collective-permute-start = (bf16[384,4096]{1,0:T(8,128)(2,1)}, bf16[384,4096]{1,0:T(8,128)(2,1)}, u32[]{:S(2)}, u32[]{:S(2)}) collective-permute-start(bf16[384,4096]{1,0:T(8,128)(2,1)} %get-tuple-element.47), channel_id=1, source_target_pairs={{0,1},{1,0},{2,3},{3,2},{4,5},{5,4},{6,7},{7,6},{8,9},{9,8},{10,11... | collective-permute-start | bytes 9437192 | tf_op jit(solution)/shard_map/ppermute | solution.py:778
  259.1 9.0 %collective-permute-start.2 = (bf16[384,1024]{1,0:T(8,128)(2,1)}, bf16[384,1024]{1,0:T(8,128)(2,1)}, u32[]{:S(2)}, u32[]{:S(2)}) collective-permute-start(bf16[384,1024]{1,0:T(8,128)(2,1)} %get-tuple-element.48), channel_id=1, source_target_pairs={{0,1},{1,0},{2,3},{3,2},{4,5},{5,4},{6,7},{7,6},{8,9},{9,8},{10,11... | collective-permute-start | bytes 2359304 | tf_op jit(solution)/shard_map/ppermute | solution.py:778
  259.2 3.4 collective-permute-start.5
  262.6 52.5 %collective-permute-start.1 = (bf16[384,512]{1,0:T(8,128)(2,1)}, bf16[384,512]{1,0:T(8,128)(2,1)}, u32[]{:S(2)}, u32[]{:S(2)}) collective-permute-start(bf16[384,512]{1,0:T(8,128)(2,1)} %get-tuple-element.80), channel_id=1, source_target_pairs={{0,1},{1,0},{2,3},{3,2},{4,5},{5,4},{6,7},{7,6},{8,9},{9,8},{10,11... | collective-permute-start | bytes 1179656 | tf_op jit(solution)/shard_map/ppermute | solution.py:779
  263.0 60.6 %collective-permute-start.6 = (bf16[384,1024]{1,0:T(8,128)(2,1)}, bf16[384,1024]{1,0:T(8,128)(2,1)}, u32[]{:S(2)}, u32[]{:S(2)}) collective-permute-start(bf16[384,1024]{1,0:T(8,128)(2,1)} %get-tuple-element.50), channel_id=1, source_target_pairs={{0,1},{1,0},{2,3},{3,2},{4,5},{5,4},{6,7},{7,6},{8,9},{9,8},{10,11... | collective-permute-start | bytes 2359304 | tf_op jit(solution)/shard_map/ppermute | solution.py:778
  263.1 4.9 copy-start.15
  301.3 2.6 copy-start.19
  301.4 2.5 copy-start.20
  303.0 20.6 %collective-permute-start.7 = (bf16[384,1536]{0,1:T(8,128)(2,1)}, bf16[384,1536]{0,1:T(8,128)(2,1)}, u32[]{:S(2)}, u32[]{:S(2)}) collective-permute-start(bf16[384,1536]{0,1:T(8,128)(2,1)} %get-tuple-element.74), channel_id=1, source_target_pairs={{0,1},{1,0},{2,3},{3,2},{4,5},{5,4},{6,7},{7,6},{8,9},{9,8},{10,11... | collective-permute-start | bytes 3538952 | tf_op jit(solution)/shard_map/ppermute | solution.py:779
  315.2 8.5 %copy-start.16 = (bf16[384,1536]{0,1:T(8,128)(2,1)S(1)}, bf16[384,1536]{0,1:T(8,128)(2,1)}, u32[]{:S(2)}) copy-start(bf16[384,1536]{0,1:T(8,128)(2,1)} %get-tuple-element.73) | copy-start | bytes 3538948
  315.2 8.5 %copy-start.33 = (bf16[384,1024]{1,0:T(8,128)(2,1)S(1)}, bf16[384,1024]{1,0:T(8,128)(2,1)}, u32[]{:S(2)}) copy-start(bf16[384,1024]{1,0:T(8,128)(2,1)} %get-tuple-element.50) | copy-start | bytes 2359300
  329.5 163.7 %copy-start.17 = (bf16[384,1024]{1,0:T(8,128)(2,1)S(1)}, bf16[384,1024]{1,0:T(8,128)(2,1)}, u32[]{:S(2)}) copy-start(bf16[384,1024]{1,0:T(8,128)(2,1)} %get-tuple-element.110) | copy-start | bytes 2359300
  488.2 5.9 %copy-start.14 = (f32[128,3072]{1,0:T(8,128)S(1)}, f32[128,3072]{1,0:T(8,128)}, u32[]{:S(2)}) copy-start(f32[128,3072]{1,0:T(8,128)} %get-tuple-element.114) | copy-start | bytes 4718596
  496.5 2.3 copy-start.12
  (22 other events, 29.8 us)
